TPU v7x, 32 devices: a whole 2x2x4 slice. The times are simulated.
32 devices in a mesh: dp: 16 (over z, y, core), tensor: 2 (over x).
Axes of the slice: x: 2, y: 2, z: 4, core: 2. Of those that a mesh axis runs over, the one named last changes fastest.
Arguments:
- source: bfloat16 [32, 1024, 512], P('dp', 'tensor'), may hold values from -6 to 6
- target: bfloat16 [32, 1024, 512], P('dp', 'tensor'), may hold values from -6 to 6
- cotangent: bfloat16 [32, 1024, 512], P('dp', 'tensor'), may hold values from -6 to 6
- lengths: int32 [32], P('dp'), may hold values from 128 to 1024, as said below
- timesteps: int32 [32], P('dp'), may hold values from 1 to 50
- masked: int32 [32, 1024], P('dp', 'tensor'), may hold values 0 or 1
- loss_mask: int32 [32, 1024], P('dp', 'tensor'), may hold values 0 or 1
- enc_query: bfloat16 [512, 512], P('dp', 'tensor'), may hold values from -0.25 to 0.25
- enc_key: bfloat16 [512, 512], P('dp', 'tensor'), may hold values from -0.25 to 0.25
- enc_value: bfloat16 [512, 512], P('dp', 'tensor'), may hold values from -0.25 to 0.25
- enc_out: bfloat16 [512, 512], P('tensor', 'dp'), may hold values from -3 to 3
- enc_up: bfloat16 [512, 2048], P('dp', 'tensor'), may hold values from -0.25 to 0.25
- enc_down: bfloat16 [2048, 512], P('tensor', 'dp'), may hold values from -0.125 to 0.125
- self_query: bfloat16 [512, 512], P('dp', 'tensor'), may hold values from -0.25 to 0.25
- self_key: bfloat16 [512, 512], P('dp', 'tensor'), may hold values from -0.25 to 0.25
- self_value: bfloat16 [512, 512], P('dp', 'tensor'), may hold values from -0.25 to 0.25
- self_out: bfloat16 [512, 512], P('tensor', 'dp'), may hold values from -3 to 3
- cross_query: bfloat16 [512, 512], P('dp', 'tensor'), may hold values from -0.25 to 0.25
- cross_key: bfloat16 [512, 512], P('dp', 'tensor'), may hold values from -0.25 to 0.25
- cross_value: bfloat16 [512, 512], P('dp', 'tensor'), may hold values from -0.25 to 0.25
- cross_out: bfloat16 [512, 512], P('tensor', 'dp'), may hold values from -3 to 3
- dec_up: bfloat16 [512, 2048], P('dp', 'tensor'), may hold values from -0.25 to 0.25
- dec_down: bfloat16 [2048, 512], P('tensor', 'dp'), may hold values from -0.125 to 0.125
- norm_gains: float32 [6, 512], replicated, may hold values from 0.1 to 1.9
- norm_shifts: float32 [6, 512], replicated, may hold values from -1.5 to 1.5
- mask_vector: float32 [512], replicated, may hold values from -4 to 4
Outputs:
- decoded: bfloat16 [32, 1024, 512], P('dp', 'tensor')
- source_grad: bfloat16 [32, 1024, 512], P('dp', 'tensor')
- target_grad: bfloat16 [32, 1024, 512], P('dp', 'tensor')
- enc_query_grad: float32 [512, 512], P('dp', 'tensor')
- enc_key_grad: float32 [512, 512], P('dp', 'tensor')
- enc_value_grad: float32 [512, 512], P('dp', 'tensor')
- enc_out_grad: float32 [512, 512], P('tensor', 'dp')
- enc_up_grad: float32 [512, 2048], P('dp', 'tensor')
- enc_down_grad: float32 [2048, 512], P('tensor', 'dp')
- self_query_grad: float32 [512, 512], P('dp', 'tensor')
- self_key_grad: float32 [512, 512], P('dp', 'tensor')
- self_value_grad: float32 [512, 512], P('dp', 'tensor')
- self_out_grad: float32 [512, 512], P('tensor', 'dp')
- cross_query_grad: float32 [512, 512], P('dp', 'tensor')
- cross_key_grad: float32 [512, 512], P('dp', 'tensor')
- cross_value_grad: float32 [512, 512], P('dp', 'tensor')
- cross_out_grad: float32 [512, 512], P('tensor', 'dp')
- dec_up_grad: float32 [512, 2048], P('dp', 'tensor')
- dec_down_grad: float32 [2048, 512], P('tensor', 'dp')
- gains_grad: float32 [6, 512], replicated
- shifts_grad: float32 [6, 512], replicated
- mask_grad: float32 [512], replicated
Inputs may be any that keep to these rules, and one draw needn't show every extreme that they name: `lengths`: among the 2 x 1 pairs of each index of dp one has all 1024 source tokens live.
All inputs are finite; a program needn't handle non-finite values. No bound on the sum of `masked` or of `loss_mask` on one device may be relied on, other than what follows from the above.
Results may differ from a plain program's by a relative error of at most 0.029.
Values may be sent and summed in bfloat16 or wider, within the bound.
A program may use at most 448 MiB of HBM per device.

v0:
```python
import jax
import jax.numpy as jnp
from jax import lax
from jax.sharding import PartitionSpec as P

HD = 64
MICRO = 2
STEPS = 50


eps = 1e-05
floor_score = -1e30


def norm_rows(inputs, gain, shift):
    average = jnp.mean(inputs, axis=-1, keepdims=True)
    centred = inputs - average
    second = jnp.mean(centred * centred, axis=-1, keepdims=True)
    return centred * lax.rsqrt(second + eps) * gain + shift


def norm_back(inputs, gain, shift, gradient):
    unused, pullback = jax.vjp(norm_rows, inputs, gain, shift)
    return pullback(gradient)


def smooth(values):
    return jax.nn.gelu(values, approximate=False)


def spread(inputs):
    return lax.all_gather(inputs.astype(jnp.bfloat16), "tensor", axis=1, tiled=True)


def collect(partial_value):
    return lax.psum_scatter(partial_value, "tensor", scatter_dimension=1, tiled=True)


def spread_grad(gradient):
    return lax.all_gather(gradient.astype(jnp.bfloat16), "tensor", axis=1, tiled=True)


def collect_grad(partial_value):
    return lax.psum_scatter(partial_value, "tensor", scatter_dimension=1, tiled=True)


def project(inputs, weight):
    return jnp.einsum("bsk,kn->bsn", inputs, weight, preferred_element_type=jnp.float32)


def weight_grad(inputs, gradient):
    return jnp.einsum("bsk,bsn->kn", inputs, gradient, preferred_element_type=jnp.float32)


def back_project(gradient, weight):
    return jnp.einsum("bsn,kn->bsk", gradient, weight, preferred_element_type=jnp.float32)


def masked_scores(query_part, key_rows, live):
    scores = jnp.einsum(
        "bqhd,bkhd->bhqk", query_part, key_rows, preferred_element_type=jnp.float32
    ) * HD ** (-0.5)
    return jnp.where(live[:, None, None, :], scores, floor_score)


def attend_forward(query_in, keys_in, w_query, w_key, w_value, live):
    pair_count, length = (query_in.shape[0], query_in.shape[1])
    head_count = w_query.shape[1] // HD
    queries = (
        project(query_in, w_query).astype(jnp.bfloat16).reshape(pair_count, length, head_count, HD)
    )
    key_rows = (
        project(keys_in, w_key).astype(jnp.bfloat16).reshape(pair_count, length, head_count, HD)
    )
    value_rows = (
        project(keys_in, w_value).astype(jnp.bfloat16).reshape(pair_count, length, head_count, HD)
    )
    block_rows = min(512, length)
    pieces = []
    totals = []
    for offset in range(0, length, block_rows):
        scores = masked_scores(queries[:, offset : offset + block_rows], key_rows, live)
        highest = jnp.max(scores, axis=-1, keepdims=True)
        exponent = jnp.exp(scores - highest)
        summed = jnp.sum(exponent, axis=-1, keepdims=True)
        softmax = (exponent / summed).astype(jnp.bfloat16)
        pieces.append(
            jnp.einsum("bhqk,bkhd->bqhd", softmax, value_rows, preferred_element_type=jnp.float32)
        )
        totals.append(highest + jnp.log(summed))
    attended = (
        jnp.concatenate(pieces, axis=1)
        .astype(jnp.bfloat16)
        .reshape(pair_count, length, head_count * HD)
    )
    return (queries, key_rows, value_rows, attended, jnp.concatenate(totals, axis=2))


def attend_backward(whole_grad, query_in, keys_in, w_query, w_key, w_value, w_out, saved, live):
    queries, key_rows, value_rows, attended, totals = saved
    pair_count, length, head_count = (queries.shape[0], queries.shape[1], queries.shape[2])
    scale_score = HD ** (-0.5)
    out_grad = weight_grad(attended, whole_grad)
    head_grad = (
        back_project(whole_grad, w_out)
        .astype(jnp.bfloat16)
        .reshape(pair_count, length, head_count, HD)
    )
    block_rows = min(512, length)
    key_total = jnp.zeros(key_rows.shape, jnp.float32)
    value_total = jnp.zeros(value_rows.shape, jnp.float32)
    query_parts = []
    for offset in range(0, length, block_rows):
        query_part = queries[:, offset : offset + block_rows]
        grad_part = head_grad[:, offset : offset + block_rows]
        scores = masked_scores(query_part, key_rows, live)
        softmax = jnp.exp(scores - totals[:, :, offset : offset + block_rows])
        value_total = value_total + jnp.einsum(
            "bhqk,bqhd->bkhd",
            softmax.astype(jnp.bfloat16),
            grad_part,
            preferred_element_type=jnp.float32,
        )
        soft_grad = jnp.einsum(
            "bqhd,bkhd->bhqk", grad_part, value_rows, preferred_element_type=jnp.float32
        )
        inner = jnp.sum(softmax * soft_grad, axis=-1, keepdims=True)
        score_grad = (softmax * (soft_grad - inner)).astype(jnp.bfloat16)
        query_parts.append(
            jnp.einsum("bhqk,bkhd->bqhd", score_grad, key_rows, preferred_element_type=jnp.float32)
            * scale_score
        )
        key_total = (
            key_total
            + jnp.einsum(
                "bhqk,bqhd->bkhd", score_grad, query_part, preferred_element_type=jnp.float32
            )
            * scale_score
        )
    query_grad = (
        jnp.concatenate(query_parts, axis=1)
        .astype(jnp.bfloat16)
        .reshape(pair_count, length, head_count * HD)
    )
    key_grad = key_total.astype(jnp.bfloat16).reshape(
        pair_count, key_rows.shape[1], head_count * HD
    )
    value_grad = value_total.astype(jnp.bfloat16).reshape(
        pair_count, value_rows.shape[1], head_count * HD
    )
    grads = (
        weight_grad(query_in, query_grad),
        weight_grad(keys_in, key_grad),
        weight_grad(keys_in, value_grad),
        out_grad,
    )
    into_keys = back_project(key_grad, w_key) + back_project(value_grad, w_value)
    return (grads, back_project(query_grad, w_query), into_keys)


def feed_forward(inputs, w_up, w_down):
    lifted = project(inputs, w_up)
    active = smooth(lifted).astype(jnp.bfloat16)
    return (lifted, active, project(active, w_down))


def feed_backward(gradient, inputs, w_up, w_down, lifted, active):
    down_grad = weight_grad(active, gradient)
    active_grad = back_project(gradient, w_down)
    unused, smooth_back = jax.vjp(smooth, lifted)
    lifted_grad = smooth_back(active_grad)[0].astype(jnp.bfloat16)
    return ((weight_grad(inputs, lifted_grad), down_grad), back_project(lifted_grad, w_up))


def body(
    source,
    target,
    cotangent,
    lengths,
    timesteps,
    masked,
    loss_mask,
    enc_query,
    enc_key,
    enc_value,
    enc_out,
    enc_up,
    enc_down,
    self_query,
    self_key,
    self_value,
    self_out,
    cross_query,
    cross_key,
    cross_value,
    cross_out,
    dec_up,
    dec_down,
    norm_gains,
    norm_shifts,
    mask_vector,
):
    pairs_dev, rows_dev = (source.shape[0], source.shape[1])
    per_micro = pairs_dev // MICRO
    seq_len = rows_dev * lax.axis_size("tensor")
    positions = jnp.arange(seq_len)
    gains, shifts = (norm_gains, norm_shifts)
    gain_total = jnp.zeros(norm_gains.shape, jnp.float32)
    shift_total = jnp.zeros(norm_shifts.shape, jnp.float32)
    mask_total = jnp.zeros(mask_vector.shape, jnp.float32)
    decoded_parts = []
    source_parts = []
    target_parts = []
    running = None
    for micro in range(MICRO):
        weights = (
            lax.all_gather(enc_query, "dp", axis=0, tiled=True),
            lax.all_gather(enc_key, "dp", axis=0, tiled=True),
            lax.all_gather(enc_value, "dp", axis=0, tiled=True),
            lax.all_gather(enc_out, "dp", axis=1, tiled=True),
            lax.all_gather(enc_up, "dp", axis=0, tiled=True),
            lax.all_gather(enc_down, "dp", axis=1, tiled=True),
            lax.all_gather(self_query, "dp", axis=0, tiled=True),
            lax.all_gather(self_key, "dp", axis=0, tiled=True),
            lax.all_gather(self_value, "dp", axis=0, tiled=True),
            lax.all_gather(self_out, "dp", axis=1, tiled=True),
            lax.all_gather(cross_query, "dp", axis=0, tiled=True),
            lax.all_gather(cross_key, "dp", axis=0, tiled=True),
            lax.all_gather(cross_value, "dp", axis=0, tiled=True),
            lax.all_gather(cross_out, "dp", axis=1, tiled=True),
            lax.all_gather(dec_up, "dp", axis=0, tiled=True),
            lax.all_gather(dec_down, "dp", axis=1, tiled=True),
        )
        wide = (
            lax.all_gather(weights[4], "tensor", axis=1, tiled=True),
            lax.all_gather(weights[5], "tensor", axis=0, tiled=True),
            lax.all_gather(weights[14], "tensor", axis=1, tiled=True),
            lax.all_gather(weights[15], "tensor", axis=0, tiled=True),
        )
        lower = micro * per_micro
        upper = lower + per_micro
        live = positions[None, :] < lengths[lower:upper][:, None]
        every = jnp.ones((per_micro, seq_len), bool)
        inputs_x = source[lower:upper].astype(jnp.float32)
        rows0 = spread(norm_rows(inputs_x, gains[0], shifts[0]))
        saved0 = attend_forward(rows0, rows0, weights[0], weights[1], weights[2], live)
        stream1 = inputs_x + collect(project(saved0[3], weights[3]))
        normed1 = norm_rows(stream1, gains[1], shifts[1])
        rows1 = normed1.astype(jnp.bfloat16)
        lifted1, active1, partial1 = feed_forward(rows1, wide[0], wide[1])
        stream2 = stream1 + partial1
        memory_rows = spread(norm_rows(stream2, gains[2], shifts[2]))
        chosen = masked[lower:upper][:, :, None] == 1
        start_y = jnp.where(chosen, mask_vector, target[lower:upper].astype(jnp.float32))
        rows3 = spread(norm_rows(start_y, gains[3], shifts[3]))
        saved3 = attend_forward(rows3, rows3, weights[6], weights[7], weights[8], every)
        stream4 = start_y + collect(project(saved3[3], weights[9]))
        rows4 = spread(norm_rows(stream4, gains[4], shifts[4]))
        saved4 = attend_forward(rows4, memory_rows, weights[10], weights[11], weights[12], live)
        stream5 = stream4 + collect(project(saved4[3], weights[13]))
        normed5 = norm_rows(stream5, gains[5], shifts[5])
        rows5 = normed5.astype(jnp.bfloat16)
        lifted5, active5, partial5 = feed_forward(rows5, wide[2], wide[3])
        stream6 = stream5 + partial5
        decoded_parts.append(stream6.astype(jnp.bfloat16))
        factor = (STEPS + 1 - timesteps[lower:upper]).astype(jnp.float32) / STEPS
        grad6 = (
            cotangent[lower:upper].astype(jnp.float32)
            * (factor[:, None] * loss_mask[lower:upper].astype(jnp.float32))[:, :, None]
        )
        (up5, down5), into5 = feed_backward(
            grad6.astype(jnp.bfloat16), rows5, wide[2], wide[3], lifted5, active5
        )
        back5 = norm_back(stream5, gains[5], shifts[5], into5)
        grad5 = grad6 + back5[0]
        grads4, query_term4, memory_term = attend_backward(
            spread_grad(grad5),
            rows4,
            memory_rows,
            weights[10],
            weights[11],
            weights[12],
            weights[13],
            saved4,
            live,
        )
        back4 = norm_back(stream4, gains[4], shifts[4], collect_grad(query_term4))
        grad4 = grad5 + back4[0]
        memory_grad = collect_grad(memory_term)
        grads3, query_term3, keys_term3 = attend_backward(
            spread_grad(grad4),
            rows3,
            rows3,
            weights[6],
            weights[7],
            weights[8],
            weights[9],
            saved3,
            every,
        )
        back3 = norm_back(start_y, gains[3], shifts[3], collect_grad(query_term3 + keys_term3))
        grad_y = grad4 + back3[0]
        target_parts.append(jnp.where(chosen, 0.0, grad_y).astype(jnp.bfloat16))
        mask_total = mask_total + jnp.sum(jnp.where(chosen, grad_y, 0.0), axis=(0, 1))
        back2 = norm_back(stream2, gains[2], shifts[2], memory_grad)
        grad2 = back2[0]
        (up1, down1), into1 = feed_backward(
            grad2.astype(jnp.bfloat16), rows1, wide[0], wide[1], lifted1, active1
        )
        back1 = norm_back(stream1, gains[1], shifts[1], into1)
        grad1 = grad2 + back1[0]
        grads0, query_term0, keys_term0 = attend_backward(
            spread_grad(grad1),
            rows0,
            rows0,
            weights[0],
            weights[1],
            weights[2],
            weights[3],
            saved0,
            live,
        )
        back0 = norm_back(inputs_x, gains[0], shifts[0], collect_grad(query_term0 + keys_term0))
        source_parts.append((grad1 + back0[0]).astype(jnp.bfloat16))
        gain_total = gain_total + jnp.stack(
            [back0[1], back1[1], back2[1], back3[1], back4[1], back5[1]]
        )
        shift_total = shift_total + jnp.stack(
            [back0[2], back1[2], back2[2], back3[2], back4[2], back5[2]]
        )
        up1, down1, up5, down5 = (
            lax.psum_scatter(
                up1.astype(jnp.bfloat16), "tensor", scatter_dimension=1, tiled=True
            ).astype(jnp.float32),
            lax.psum_scatter(
                down1.astype(jnp.bfloat16), "tensor", scatter_dimension=0, tiled=True
            ).astype(jnp.float32),
            lax.psum_scatter(
                up5.astype(jnp.bfloat16), "tensor", scatter_dimension=1, tiled=True
            ).astype(jnp.float32),
            lax.psum_scatter(
                down5.astype(jnp.bfloat16), "tensor", scatter_dimension=0, tiled=True
            ).astype(jnp.float32),
        )
        fresh = (
            grads0[0],
            grads0[1],
            grads0[2],
            grads0[3],
            up1,
            down1,
            grads3[0],
            grads3[1],
            grads3[2],
            grads3[3],
            grads4[0],
            grads4[1],
            grads4[2],
            grads4[3],
            up5,
            down5,
        )
        running = fresh if micro == 0 else jax.tree.map(jnp.add, running, tuple(fresh))
    running = (
        lax.psum_scatter(
            running[0].astype(jnp.bfloat16), "dp", scatter_dimension=0, tiled=True
        ).astype(jnp.float32),
        lax.psum_scatter(
            running[1].astype(jnp.bfloat16), "dp", scatter_dimension=0, tiled=True
        ).astype(jnp.float32),
        lax.psum_scatter(
            running[2].astype(jnp.bfloat16), "dp", scatter_dimension=0, tiled=True
        ).astype(jnp.float32),
        lax.psum_scatter(
            running[3].astype(jnp.bfloat16), "dp", scatter_dimension=1, tiled=True
        ).astype(jnp.float32),
        lax.psum_scatter(
            running[4].astype(jnp.bfloat16), "dp", scatter_dimension=0, tiled=True
        ).astype(jnp.float32),
        lax.psum_scatter(
            running[5].astype(jnp.bfloat16), "dp", scatter_dimension=1, tiled=True
        ).astype(jnp.float32),
        lax.psum_scatter(
            running[6].astype(jnp.bfloat16), "dp", scatter_dimension=0, tiled=True
        ).astype(jnp.float32),
        lax.psum_scatter(
            running[7].astype(jnp.bfloat16), "dp", scatter_dimension=0, tiled=True
        ).astype(jnp.float32),
        lax.psum_scatter(
            running[8].astype(jnp.bfloat16), "dp", scatter_dimension=0, tiled=True
        ).astype(jnp.float32),
        lax.psum_scatter(
            running[9].astype(jnp.bfloat16), "dp", scatter_dimension=1, tiled=True
        ).astype(jnp.float32),
        lax.psum_scatter(
            running[10].astype(jnp.bfloat16), "dp", scatter_dimension=0, tiled=True
        ).astype(jnp.float32),
        lax.psum_scatter(
            running[11].astype(jnp.bfloat16), "dp", scatter_dimension=0, tiled=True
        ).astype(jnp.float32),
        lax.psum_scatter(
            running[12].astype(jnp.bfloat16), "dp", scatter_dimension=0, tiled=True
        ).astype(jnp.float32),
        lax.psum_scatter(
            running[13].astype(jnp.bfloat16), "dp", scatter_dimension=1, tiled=True
        ).astype(jnp.float32),
        lax.psum_scatter(
            running[14].astype(jnp.bfloat16), "dp", scatter_dimension=0, tiled=True
        ).astype(jnp.float32),
        lax.psum_scatter(
            running[15].astype(jnp.bfloat16), "dp", scatter_dimension=1, tiled=True
        ).astype(jnp.float32),
    )
    vectors = lax.psum((gain_total, shift_total, mask_total), ("dp", "tensor"))
    return (
        jnp.concatenate(decoded_parts, axis=0),
        jnp.concatenate(source_parts, axis=0),
        jnp.concatenate(target_parts, axis=0),
        running[0],
        running[1],
        running[2],
        running[3],
        running[4],
        running[5],
        running[6],
        running[7],
        running[8],
        running[9],
        running[10],
        running[11],
        running[12],
        running[13],
        running[14],
        running[15],
        vectors[0],
        vectors[1],
        vectors[2],
    )


def solution(mesh):
    return jax.shard_map(
        body,
        mesh=mesh,
        in_specs=(
            P("dp", "tensor", None),
            P("dp", "tensor", None),
            P("dp", "tensor", None),
            P("dp"),
            P("dp"),
            P("dp", "tensor"),
            P("dp", "tensor"),
            P("dp", "tensor"),
            P("dp", "tensor"),
            P("dp", "tensor"),
            P("tensor", "dp"),
            P("dp", "tensor"),
            P("tensor", "dp"),
            P("dp", "tensor"),
            P("dp", "tensor"),
            P("dp", "tensor"),
            P("tensor", "dp"),
            P("dp", "tensor"),
            P("dp", "tensor"),
            P("dp", "tensor"),
            P("tensor", "dp"),
            P("dp", "tensor"),
            P("tensor", "dp"),
            P(),
            P(),
            P(),
        ),
        out_specs=(
            P("dp", "tensor", None),
            P("dp", "tensor", None),
            P("dp", "tensor", None),
            P("dp", "tensor"),
            P("dp", "tensor"),
            P("dp", "tensor"),
            P("tensor", "dp"),
            P("dp", "tensor"),
            P("tensor", "dp"),
            P("dp", "tensor"),
            P("dp", "tensor"),
            P("dp", "tensor"),
            P("tensor", "dp"),
            P("dp", "tensor"),
            P("dp", "tensor"),
            P("dp", "tensor"),
            P("tensor", "dp"),
            P("dp", "tensor"),
            P("tensor", "dp"),
            P(),
            P(),
            P(),
        ),
        check_vma=False,
    )
```

profile of v0, /device:TPU:0, one launch (start us, length us, event | category | flops | bytes accessed | tf_op | source)
XLA Modules:
  0.0 2419.0 jit_solution(13346469123481206825)
XLA Ops:
  28.7 23.8 all_gather.129
  315.5 34.1 %reduce-scatter.45.cloned.1.call-done = f32[1,512,512]{2,1,0:T(8,128)} async-done(((f32[1,1024,512]{2,1,0:T(8,128)}), f32[1,512,512]{2,1,0:T(8,128)}) %reduce-scatter.45.cloned.1.call-update) | async-done | bytes 1048592 | tf_op jit(solution)/shard_map/reduce_scatter | solution.py:36
  355.4 28.8 %all-gather.29.cloned.1.call-done = bf16[512,2048]{1,0:T(8,128)(2,1)} async-done(((bf16[512,1024]{1,0:T(8,128)(2,1)}), bf16[512,2048]{1,0:T(8,128)(2,1)}) %all-gather.29.cloned.1.call-update) | async-done | bytes 2097168 | tf_op jit(solution)/shard_map/all_gather | solution.py:235
  441.4 22.0 all_gather.139
  589.5 32.9 %reduce-scatter.53.cloned.1.call-done = f32[1,512,512]{2,1,0:T(8,128)} async-done(((f32[1,1024,512]{2,1,0:T(8,128)}), f32[1,512,512]{2,1,0:T(8,128)}) %reduce-scatter.53.cloned.1.call-update) | async-done | bytes 1048592 | tf_op jit(solution)/shard_map/reduce_scatter | solution.py:36
  625.1 31.4 %reduce-scatter.47.cloned.1.call-done = f32[1,512,512]{2,1,0:T(8,128)} async-done(((f32[1,1024,512]{2,1,0:T(8,128)}), f32[1,512,512]{2,1,0:T(8,128)}) %reduce-scatter.47.cloned.1.call-update) | async-done | bytes 1048592 | tf_op jit(solution)/shard_map/reduce_scatter | solution.py:36
  658.2 33.0 %all-gather.41.cloned.1.call-done = bf16[512,2048]{1,0:T(8,128)(2,1)} async-done(((bf16[512,1024]{1,0:T(8,128)(2,1)}), bf16[512,2048]{1,0:T(8,128)(2,1)}) %all-gather.41.cloned.1.call-update) | async-done | bytes 2097168 | tf_op jit(solution)/shard_map/all_gather | solution.py:237
  822.8 21.4 reduce-scatter.63.cloned.1.call-done
  943.2 31.4 %reduce-scatter.59.cloned.1.call-done = f32[1,512,512]{2,1,0:T(8,128)} async-done(((f32[1,1024,512]{2,1,0:T(8,128)}), f32[1,512,512]{2,1,0:T(8,128)}) %reduce-scatter.59.cloned.1.call-update) | async-done | bytes 1048592 | tf_op jit(solution)/shard_map/reduce_scatter | solution.py:44
  1015.2 27.6 %reduce-scatter.113.cloned.1.call-done = bf16[1024,512]{1,0:T(8,128)(2,1)} async-done(((bf16[2048,512]{1,0:T(8,128)(2,1)}), bf16[1024,512]{1,0:T(8,128)(2,1)}) %reduce-scatter.113.cloned.1.call-update) | async-done | bytes 1048592 | tf_op jit(solution)/shard_map/reduce_scatter | solution.py:341
  1053.8 23.0 reduce-scatter.105.cloned.1.call-done
  1076.9 34.2 %reduce-scatter.107.cloned.1.call-done = bf16[512,1024]{1,0:T(8,128)(2,1)} async-done(((bf16[512,2048]{1,0:T(8,128)(2,1)}), bf16[512,1024]{1,0:T(8,128)(2,1)}) %reduce-scatter.107.cloned.1.call-update) | async-done | bytes 1048592 | tf_op jit(solution)/shard_map/reduce_scatter | solution.py:338
  1410.5 39.4 %reduce-scatter.103.cloned.1.call-done = bf16[256,32]{0,1:T(8,128)(2,1)} async-done(((bf16[256,512]{0,1:T(8,128)(2,1)}), bf16[256,32]{0,1:T(8,128)(2,1)}) %reduce-scatter.103.cloned.1.call-update) | async-done | bytes 16400 | tf_op jit(solution)/shard_map/reduce_scatter | solution.py:404
  1451.2 56.6 %reduce-scatter.101.cloned.1.call-done = bf16[32,256]{1,0:T(8,128)(2,1)} async-done(((bf16[512,256]{1,0:T(8,128)(2,1)}), bf16[32,256]{1,0:T(8,128)(2,1)}) %reduce-scatter.101.cloned.1.call-update) | async-done | bytes 16400 | tf_op jit(solution)/shard_map/reduce_scatter | solution.py:401
  1509.1 56.4 %reduce-scatter.99.cloned.1.call-done = bf16[32,256]{1,0:T(8,128)(2,1)} async-done(((bf16[512,256]{1,0:T(8,128)(2,1)}), bf16[32,256]{1,0:T(8,128)(2,1)}) %reduce-scatter.99.cloned.1.call-update) | async-done | bytes 16400 | tf_op jit(solution)/shard_map/reduce_scatter | solution.py:398
  1566.8 56.5 %reduce-scatter.97.cloned.1.call-done = bf16[32,256]{1,0:T(8,128)(2,1)} async-done(((bf16[512,256]{1,0:T(8,128)(2,1)}), bf16[32,256]{1,0:T(8,128)(2,1)}) %reduce-scatter.97.cloned.1.call-update) | async-done | bytes 16400 | tf_op jit(solution)/shard_map/reduce_scatter | solution.py:395
  1626.2 54.8 %reduce-scatter.95.cloned.1.call-done = bf16[256,32]{0,1:T(8,128)(2,1)} async-done(((bf16[256,512]{0,1:T(8,128)(2,1)}), bf16[256,32]{0,1:T(8,128)(2,1)}) %reduce-scatter.95.cloned.1.call-update) | async-done | bytes 16400 | tf_op jit(solution)/shard_map/reduce_scatter | solution.py:392
  1682.4 56.4 %reduce-scatter.93.cloned.1.call-done = bf16[32,256]{1,0:T(8,128)(2,1)} async-done(((bf16[512,256]{1,0:T(8,128)(2,1)}), bf16[32,256]{1,0:T(8,128)(2,1)}) %reduce-scatter.93.cloned.1.call-update) | async-done | bytes 16400 | tf_op jit(solution)/shard_map/reduce_scatter | solution.py:389
  1740.1 56.4 %reduce-scatter.77.cloned.1.call-done = bf16[256,32]{0,1:T(8,128)(2,1)} async-done(((bf16[256,512]{0,1:T(8,128)(2,1)}), bf16[256,32]{0,1:T(8,128)(2,1)}) %reduce-scatter.77.cloned.1.call-update) | async-done | bytes 16400 | tf_op jit(solution)/shard_map/reduce_scatter | solution.py:374
  1797.9 56.3 %reduce-scatter.75.cloned.1.call-done = bf16[32,256]{1,0:T(8,128)(2,1)} async-done(((bf16[512,256]{1,0:T(8,128)(2,1)}), bf16[32,256]{1,0:T(8,128)(2,1)}) %reduce-scatter.75.cloned.1.call-update) | async-done | bytes 16400 | tf_op jit(solution)/shard_map/reduce_scatter | solution.py:371
  1855.5 56.4 %reduce-scatter.71.cloned.1.call-done = bf16[32,256]{1,0:T(8,128)(2,1)} async-done(((bf16[512,256]{1,0:T(8,128)(2,1)}), bf16[32,256]{1,0:T(8,128)(2,1)}) %reduce-scatter.71.cloned.1.call-update) | async-done | bytes 16400 | tf_op jit(solution)/shard_map/reduce_scatter | solution.py:365
  1913.3 56.5 %reduce-scatter.73.cloned.1.call-done = bf16[32,256]{1,0:T(8,128)(2,1)} async-done(((bf16[512,256]{1,0:T(8,128)(2,1)}), bf16[32,256]{1,0:T(8,128)(2,1)}) %reduce-scatter.73.cloned.1.call-update) | async-done | bytes 16400 | tf_op jit(solution)/shard_map/reduce_scatter | solution.py:368
  1971.2 56.5 %reduce-scatter.89.cloned.1.call-done = bf16[32,256]{1,0:T(8,128)(2,1)} async-done(((bf16[512,256]{1,0:T(8,128)(2,1)}), bf16[32,256]{1,0:T(8,128)(2,1)}) %reduce-scatter.89.cloned.1.call-update) | async-done | bytes 16400 | tf_op jit(solution)/shard_map/reduce_scatter | solution.py:383
  2029.0 56.5 %reduce-scatter.91.cloned.1.call-done = bf16[32,256]{1,0:T(8,128)(2,1)} async-done(((bf16[512,256]{1,0:T(8,128)(2,1)}), bf16[32,256]{1,0:T(8,128)(2,1)}) %reduce-scatter.91.cloned.1.call-update) | async-done | bytes 16400 | tf_op jit(solution)/shard_map/reduce_scatter | solution.py:386
  2086.8 31.6 %reduce-scatter.79.cloned.1.call-done = bf16[512,1024]{1,0:T(8,128)(2,1)} async-done(((bf16[512,2048]{1,0:T(8,128)(2,1)}), bf16[512,1024]{1,0:T(8,128)(2,1)}) %reduce-scatter.79.cloned.1.call-update) | async-done | bytes 1048592 | tf_op jit(solution)/shard_map/reduce_scatter | solution.py:332
  2118.5 34.2 %reduce-scatter.81.cloned.1.call-done = bf16[512,1024]{1,0:T(8,128)(2,1)} async-done(((bf16[512,2048]{1,0:T(8,128)(2,1)}), bf16[512,1024]{1,0:T(8,128)(2,1)}) %reduce-scatter.81.cloned.1.call-update) | async-done | bytes 1048592 | tf_op jit(solution)/shard_map/reduce_scatter | solution.py:332
  2155.6 31.2 %reduce-scatter.61.cloned.1.call-done = f32[1,512,512]{2,1,0:T(8,128)} async-done(((f32[1,1024,512]{2,1,0:T(8,128)}), f32[1,512,512]{2,1,0:T(8,128)}) %reduce-scatter.61.cloned.1.call-update) | async-done | bytes 1048592 | tf_op jit(solution)/shard_map/reduce_scatter | solution.py:44
  2186.8 34.2 %reduce-scatter.57.cloned.1.call-done = f32[1,512,512]{2,1,0:T(8,128)} async-done(((f32[1,1024,512]{2,1,0:T(8,128)}), f32[1,512,512]{2,1,0:T(8,128)}) %reduce-scatter.57.cloned.1.call-update) | async-done | bytes 1048592 | tf_op jit(solution)/shard_map/reduce_scatter | solution.py:44
  2223.2 31.9 %reduce-scatter.65.cloned.1.call-done = f32[1,512,512]{2,1,0:T(8,128)} async-done(((f32[1,1024,512]{2,1,0:T(8,128)}), f32[1,512,512]{2,1,0:T(8,128)}) %reduce-scatter.65.cloned.1.call-update) | async-done | bytes 1048592 | tf_op jit(solution)/shard_map/reduce_scatter | solution.py:44
  2255.1 34.0 %reduce-scatter.69.cloned.1.call-done = f32[1,512,512]{2,1,0:T(8,128)} async-done(((f32[1,1024,512]{2,1,0:T(8,128)}), f32[1,512,512]{2,1,0:T(8,128)}) %reduce-scatter.69.cloned.1.call-update) | async-done | bytes 1048592 | tf_op jit(solution)/shard_map/reduce_scatter | solution.py:44
  2300.1 40.4 %all-reduce = (f32[6,512]{1,0:T(8,128)}, f32[6,512]{1,0:T(8,128)}, f32[512]{0:T(512)}) all-reduce(f32[6,512]{1,0:T(8,128)S(1)} %add.765, f32[6,512]{1,0:T(8,128)S(1)} %add.766, f32[512]{0:T(512)S(1)} %add.767), channel_id=1, replica_groups=mesh['dp'=16,'tensor'=2] {'dp','tensor'}, use_global_device_ids=true, to_apply=%region_134.135 | all-reduce | flops 6656 | bytes 53248 | tf_op jit(solution)/shard_map/psum | solution.py:414
  2351.8 58.7 %reduce-scatter.83.cloned.1.call-done = bf16[32,1024]{1,0:T(8,128)(2,1)} async-done(((bf16[512,1024]{1,0:T(8,128)(2,1)}), bf16[32,1024]{1,0:T(8,128)(2,1)}) %reduce-scatter.83.cloned.1.call-update) | async-done | bytes 65552 | tf_op jit(solution)/shard_map/reduce_scatter | solution.py:377
  (1347 shorter events, 1098.2 us)
Async XLA Ops:
  23.8 238.5 %all-gather.25.cloned.1.call-start = ((), (), s32[]{:S(2)}) async-start(), calls=%async_computation.40 | async-start | bytes 1572864 | tf_op jit(solution)/shard_map/all_gather | solution.py:32
  24.4 266.6 %all-gather.27.cloned.1.call-start = ((), (), s32[]{:S(2)}) async-start(), calls=%async_computation.42 | async-start | bytes 1114112 | tf_op jit(solution)/shard_map/all_gather | solution.py:221
  25.0 266.8 %all-gather.31.cloned.1.call-start = ((), (), s32[]{:S(2)}) async-start(), calls=%async_computation.44 | async-start | bytes 1114112 | tf_op jit(solution)/shard_map/all_gather | solution.py:222
  25.5 266.8 %reduce-scatter.43.cloned.1.call-start = ((), (), s32[]{:S(2)}) async-start(), calls=%async_computation.39 | async-start | bytes 3145728 | tf_op jit(solution)/shard_map/reduce_scatter | solution.py:36
  292.3 227.1 %all-gather.53.cloned.1.call-start = ((), (), s32[]{:S(2)}) async-start(), calls=%async_computation.58 | async-start | bytes 1572864 | tf_op jit(solution)/shard_map/all_gather | solution.py:32
  942.9 255.5 %all-gather.65.cloned.1.call-start = ((), (), s32[]{:S(2)}) async-start(), calls=%async_computation.72 | async-start | bytes 1572864 | tf_op jit(solution)/shard_map/all_gather | solution.py:40
  990.3 228.0 %all-gather.61.cloned.1.call-start = ((), (), s32[]{:S(2)}) async-start(), calls=%async_computation.66 | async-start | bytes 1572864 | tf_op jit(solution)/shard_map/all_gather | solution.py:40
  1002.0 228.4 %all-gather.57.cloned.1.call-start = ((), (), s32[]{:S(2)}) async-start(), calls=%async_computation.62 | async-start | bytes 1572864 | tf_op jit(solution)/shard_map/all_gather | solution.py:40
  1005.8 390.0 %reduce-scatter.87.cloned.1.call-start = ((), (), s32[]{:S(2)}) async-start(), calls=%async_computation.82 | async-start | bytes 3145728 | tf_op jit(solution)/shard_map/reduce_scatter | solution.py:335
  1010.3 385.5 %reduce-scatter.85.cloned.1.call-start = ((), (), s32[]{:S(2)}) async-start(), calls=%async_computation.81 | async-start | bytes 3145728 | tf_op jit(solution)/shard_map/reduce_scatter | solution.py:335
  1014.6 392.5 %reduce-scatter.117.cloned.1.call-start = ((), (), s32[]{:S(2)}) async-start(), calls=%async_computation.97 | async-start | bytes 1114112
  1045.9 363.0 %reduce-scatter.109.cloned.1.call-start = ((), (), s32[]{:S(2)}) async-start(), calls=%async_computation.93 | async-start | bytes 1114112 | tf_op jit(solution)/shard_map/reduce_scatter | solution.py:407
  1114.0 335.9 %reduce-scatter.103.cloned.1.call-start = ((), (), s32[]{:S(2)}) async-start(), calls=%async_computation.90 | async-start | bytes 278528 | tf_op jit(solution)/shard_map/reduce_scatter | solution.py:404
  1165.1 342.7 %reduce-scatter.101.cloned.1.call-start = ((), (), s32[]{:S(2)}) async-start(), calls=%async_computation.89 | async-start | bytes 278528 | tf_op jit(solution)/shard_map/reduce_scatter | solution.py:401
  1180.4 385.1 %reduce-scatter.99.cloned.1.call-start = ((), (), s32[]{:S(2)}) async-start(), calls=%async_computation.88 | async-start | bytes 278528 | tf_op jit(solution)/shard_map/reduce_scatter | solution.py:398
  1184.8 438.6 %reduce-scatter.97.cloned.1.call-start = ((), (), s32[]{:S(2)}) async-start(), calls=%async_computation.87 | async-start | bytes 278528 | tf_op jit(solution)/shard_map/reduce_scatter | solution.py:395
  1190.5 490.5 %reduce-scatter.95.cloned.1.call-start = ((), (), s32[]{:S(2)}) async-start(), calls=%async_computation.86 | async-start | bytes 278528 | tf_op jit(solution)/shard_map/reduce_scatter | solution.py:392
  1318.4 420.4 %reduce-scatter.93.cloned.1.call-start = ((), (), s32[]{:S(2)}) async-start(), calls=%async_computation.85 | async-start | bytes 278528 | tf_op jit(solution)/shard_map/reduce_scatter | solution.py:389
  1323.9 472.6 %reduce-scatter.77.cloned.1.call-start = ((), (), s32[]{:S(2)}) async-start(), calls=%async_computation.77 | async-start | bytes 278528 | tf_op jit(solution)/shard_map/reduce_scatter | solution.py:374
  1331.4 522.8 %reduce-scatter.75.cloned.1.call-start = ((), (), s32[]{:S(2)}) async-start(), calls=%async_computation.76 | async-start | bytes 278528 | tf_op jit(solution)/shard_map/reduce_scatter | solution.py:371
  1339.5 572.5 %reduce-scatter.71.cloned.1.call-start = ((), (), s32[]{:S(2)}) async-start(), calls=%async_computation.74 | async-start | bytes 278528 | tf_op jit(solution)/shard_map/reduce_scatter | solution.py:365
  1347.6 622.2 %reduce-scatter.73.cloned.1.call-start = ((), (), s32[]{:S(2)}) async-start(), calls=%async_computation.75 | async-start | bytes 278528 | tf_op jit(solution)/shard_map/reduce_scatter | solution.py:368
  1362.5 665.2 %reduce-scatter.89.cloned.1.call-start = ((), (), s32[]{:S(2)}) async-start(), calls=%async_computation.83 | async-start | bytes 278528 | tf_op jit(solution)/shard_map/reduce_scatter | solution.py:383
  1366.8 718.7 %reduce-scatter.91.cloned.1.call-start = ((), (), s32[]{:S(2)}) async-start(), calls=%async_computation.84 | async-start | bytes 278528 | tf_op jit(solution)/shard_map/reduce_scatter | solution.py:386
  1372.3 746.1 %reduce-scatter.79.cloned.1.call-start = ((), (), s32[]{:S(2)}) async-start(), calls=%async_computation.78 | async-start | bytes 3145728 | tf_op jit(solution)/shard_map/reduce_scatter | solution.py:332
  1376.8 775.8 %reduce-scatter.81.cloned.1.call-start = ((), (), s32[]{:S(2)}) async-start(), calls=%async_computation.79 | async-start | bytes 3145728 | tf_op jit(solution)/shard_map/reduce_scatter | solution.py:332
  1381.3 805.5 %reduce-scatter.61.cloned.1.call-start = ((), (), s32[]{:S(2)}) async-start(), calls=%async_computation.67 | async-start | bytes 3145728 | tf_op jit(solution)/shard_map/reduce_scatter | solution.py:44
  1385.3 835.6 %reduce-scatter.57.cloned.1.call-start = ((), (), s32[]{:S(2)}) async-start(), calls=%async_computation.63 | async-start | bytes 3145728 | tf_op jit(solution)/shard_map/reduce_scatter | solution.py:44
  1388.7 866.4 %reduce-scatter.65.cloned.1.call-start = ((), (), s32[]{:S(2)}) async-start(), calls=%async_computation.70 | async-start | bytes 3145728 | tf_op jit(solution)/shard_map/reduce_scatter | solution.py:44
  1392.3 896.9 %reduce-scatter.69.cloned.1.call-start = ((), (), s32[]{:S(2)}) async-start(), calls=%async_computation.73 | async-start | bytes 3145728 | tf_op jit(solution)/shard_map/reduce_scatter | solution.py:44
  1395.7 954.4 %reduce-scatter.115.cloned.1.call-start = ((), (), s32[]{:S(2)}) async-start(), calls=%async_computation.96 | async-start | bytes 1114112
  1399.1 1011.4 %reduce-scatter.83.cloned.1.call-start = ((), (), s32[]{:S(2)}) async-start(), calls=%async_computation.80 | async-start | bytes 1114112 | tf_op jit(solution)/shard_map/reduce_scatter | solution.py:377
  (448 other events, 19201.7 us)
Sparse Core Ops, SparseCore 0:
  116.0 38.0 all-gather.26
  156.0 36.8 all-gather.30
  283.5 31.8 reduce-scatter.50
  317.7 31.8 reduce-scatter.44
  351.1 33.1 all-gather.28
  385.6 33.1 all-gather.32
  512.5 37.9 all-gather.38
  552.5 36.8 all-gather.42
  658.0 33.1 all-gather.40
  692.7 33.1 all-gather.44
  873.8 31.8 reduce-scatter.54
  908.1 32.2 reduce-scatter.66
  976.8 31.8 reduce-scatter.110
  1045.0 31.8 reduce-scatter.104
  1274.0 57.3 reduce-scatter.116
  1335.4 56.4 reduce-scatter.108
  1395.5 54.3 reduce-scatter.102
  1453.4 54.3 reduce-scatter.100
  1511.1 54.3 reduce-scatter.98
  1569.0 54.2 reduce-scatter.96
  1626.7 54.2 reduce-scatter.94
  1684.4 54.2 reduce-scatter.92
  1742.1 54.3 reduce-scatter.76
  1799.9 54.2 reduce-scatter.74
  1857.6 54.3 reduce-scatter.70
  1915.5 54.3 reduce-scatter.72
  1973.2 54.3 reduce-scatter.88
  2031.2 54.2 reduce-scatter.90
  2154.9 31.8 reduce-scatter.60
  2223.2 31.8 reduce-scatter.64
  2292.6 57.3 reduce-scatter.114
  2354.1 56.3 reduce-scatter.82
  (28 shorter events, 741.2 us)
where the time goes:
time: 2430 us; the launch traced here: 2420 us
  waiting for transfers between devices  1350 us (56%)
  matrix products  532 us (22%)
  blocking collectives  275 us (11%)
  other arithmetic  194 us (8%)
  local copies, waits for them, and re-layouts  38.3 us (2%)
    reduce_scatter x8, waiting for transfers between devices, collect_grad(): lax.psum_scatter(partial_value, 'tensor', scatter_dimension=1, tiled=True)  184 us
    reduce_scatter x6, waiting for transfers between devices, collect(): lax.psum_scatter(partial_value, 'tensor', scatter_dimension=1, tiled=True)  118 us
    dot_general x32, matrix products, project(): jnp.einsum('bsk,kn->bsn', inputs, weight, preferred_element_type=jnp.floa...  98.8 us
    dot_general x12, matrix products, attend_backward(): jnp.einsum('bqhd,bkhd->bhqk', grad_part, value_rows, preferred_element_ty...  89 us
    dot_general x32, matrix products, weight_grad(): jnp.einsum('bsk,bsn->kn', inputs, gradient, preferred_element_type=jnp.fl...  73.7 us
    convert_element_type x8, other arithmetic, attend_backward(): score_grad = (softmax * (soft_grad - inner)).astype(jnp.bfloat16)  66.1 us
    reduce_scatter x2, waiting for transfers between devices, body(): lax.psum_scatter(up1.astype(jnp.bfloat16), 'tensor', scatter_dimension=1,...  65.8 us
    dot_general x32, matrix products, back_project(): jnp.einsum('bsn,kn->bsk', gradient, weight, preferred_element_type=jnp.fl...  61.3 us
  transfers between devices with their start and end apart: 60, of which 37 were waited for; matrix products, arithmetic and copies ran while one was open for 27% of the time, Pallas kernels for 0%

commit v1 on v0

--- a/solution.py
+++ b/solution.py
@@ -1,6 +1,8 @@
 import jax
 import jax.numpy as jnp
 from jax import lax
+from jax.experimental import pallas as pl
+from jax.experimental.pallas import tpu as pltpu
 from jax.sharding import PartitionSpec as P
 
 HD = 64
@@ -438,9 +440,934 @@
     )
 
 
+F32 = jnp.float32
+BF = jnp.bfloat16
+LOG2E = 1.4426950408889634
+LN2 = 0.6931471805599453
+NN = (((1,), (0,)), ((), ()))
+NT = (((1,), (1,)), ((), ()))
+MESH = pl.DeviceIdType.MESH
+RB = 256
+VMEM_LIMIT = 62 * 2**20
+
+
+def dg(left, right, dims=NN):
+    return lax.dot_general(left, right, dims, preferred_element_type=F32)
+
+
+def ln_hat(x):
+    centred = x - jnp.mean(x, axis=-1, keepdims=True)
+    rstd = lax.rsqrt(jnp.mean(centred * centred, axis=-1, keepdims=True) + eps)
+    return centred * rstd, rstd
+
+
+def ln_back(x, gain, gradient):
+    hat, rstd = ln_hat(x)
+    scaled = gradient * gain
+    first = jnp.mean(scaled, axis=-1, keepdims=True)
+    second = jnp.mean(scaled * hat, axis=-1, keepdims=True)
+    dx = rstd * (scaled - first - hat * second)
+    dgain = jnp.sum(gradient * hat, axis=0, keepdims=True)
+    dshift = jnp.sum(gradient, axis=0, keepdims=True)
+    return dx, dgain, dshift
+
+
+def gelu_both(u):
+    size = jnp.abs(u)
+    t = 1.0 / (1.0 + (0.3275911 * 0.7071067811865476) * size)
+    ex = jnp.exp2(u * u * (-0.5 * LOG2E))
+    poly = t * (
+        0.127414796
+        + t * (-0.142248368 + t * (0.7107068705 + t * (-0.7265760135 + t * 0.5307027145)))
+    )
+    tail = poly * ex
+    phi = jnp.where(u > 0, 1.0 - tail, tail)
+    return u * phi, phi + u * ex * 0.3989422804014327
+
+
+def rows_loop(total, step, run):
+    def once(i, carry):
+        run(pl.ds(pl.multiple_of(i * step, step), step))
+        return carry
+
+    lax.fori_loop(0, total // step, once, 0)
+
+
+def load_weight(w_hbm, offset, width, dst, sems, base):
+    copies = []
+    for t in range(2):
+        cp = pltpu.make_async_copy(
+            w_hbm.at[t, :, pl.ds(offset, width)],
+            dst.at[:, pl.ds(t * width, width)],
+            sems.at[base + t],
+        )
+        cp.start()
+        copies.append(cp)
+    return copies
+
+
+def store_grad(src, g_hbm, offset, width, sems, base):
+    copies = []
+    for t in range(2):
+        cp = pltpu.make_async_copy(
+            src.at[:, pl.ds(t * width, width)],
+            g_hbm.at[t, :, pl.ds(offset, width)],
+            sems.at[base + t],
+        )
+        cp.start()
+        copies.append(cp)
+    return copies
+
+
+def wait_all(copies):
+    for cp in copies:
+        cp.wait()
+
+
+def attn_project(x, gain, shift, kv, wq, wk, wv, a, q, k, v):
+    def run(sl):
+        hat, unused = ln_hat(x[sl, :].astype(F32))
+        rows = (hat * gain + shift).astype(BF)
+        a[sl, :] = rows
+        q[sl, :] = (dg(rows, wq[...]) * (LOG2E * HD**-0.5)).astype(BF)
+        keys_in = rows if kv is None else kv[sl, :]
+        k[sl, :] = dg(keys_in, wk[...]).astype(BF)
+        v[sl, :] = dg(keys_in, wv[...]).astype(BF)
+
+    rows_loop(x.shape[0], RB, run)
+
+
+def attn_core(length, q, k, v, o, ol, r, e_hbm, ebuf, esem):
+    seq = q.shape[0]
+    pairs = q.shape[1] // 128
+    block = 512
+    lane = lax.broadcasted_iota(jnp.int32, (1, 128), 1)
+    low = lane < 64
+    one = jnp.ones((), BF)
+    key = lax.broadcasted_iota(jnp.int32, (seq, 1), 0)
+    bias = jnp.where(key < length, 0.0, floor_score).astype(F32)
+
+    def out(head, h, b):
+        sl = pl.ds(b * block, block)
+        return pltpu.make_async_copy(ebuf.at[h, sl, :], e_hbm.at[head, sl, :], esem.at[h, b])
+
+    def pair(p, carry):
+        cols = pl.ds(pl.multiple_of(p * 128, 128), 128)
+        kp = k[:, cols].astype(F32)
+        vp = v[:, cols]
+        parts = []
+        for h in range(2):
+            if h == 0:
+                ka = jnp.where(low, kp, jnp.where(lane == 64, bias, 0.0)).astype(BF)
+                va = jnp.where(low, vp, one)
+            else:
+                ka = jnp.where(low, jnp.where(lane == 0, bias, 0.0), kp).astype(BF)
+                va = jnp.where(low, one, vp)
+            for b in range(seq // block):
+                sl = pl.ds(b * block, block)
+
+                @pl.when(p > 0)
+                def unused_wait():
+                    out(2 * p - 2 + h, h, b).wait()
+
+                qp = q[sl, cols]
+                qm = jnp.where(low, qp, one) if h == 0 else jnp.where(low, one, qp)
+                s = dg(qm, ka, NT)
+                e = jnp.exp2(s - jnp.max(s, axis=-1, keepdims=True)).astype(BF)
+                ebuf[h, sl, :] = e
+                out(2 * p + h, h, b).start()
+                parts.append(dg(e, va))
+        for b in range(seq // block):
+            sl = pl.ds(b * block, block)
+            first, second = parts[b], parts[seq // block + b]
+            un = jnp.where(low, first, second)
+            sums = pltpu.roll(jnp.where(low, second, first), 64, 1)
+            inverse = 1.0 / sums
+            r[sl, cols] = inverse.astype(BF)
+            joined = un * inverse
+            rounded = joined.astype(BF)
+            o[sl, cols] = rounded
+            ol[sl, cols] = (joined - rounded.astype(F32)).astype(BF)
+        return carry
+
+    lax.fori_loop(0, pairs, pair, 0)
+    for h in range(2):
+        for b in range(seq // block):
+            out(2 * pairs - 2 + h, h, b).wait()
+
+
+def attn_join(x, o, wo, y):
+    def run(sl):
+        y[sl, :] = x[sl, :].astype(F32) + dg(o[sl, :], wo[...], NT)
+
+    rows_loop(x.shape[0], RB, run)
+
+
+def attn_back_core(q, k, v, do, o, ol, e_hbm, ebuf, esem, ds, dq, dk, dv):
+    seq = q.shape[0]
+    heads = e_hbm.shape[0]
+    block = 512
+    lane = lax.broadcasted_iota(jnp.int32, (1, 128), 1)
+    low = lane < 64
+    zero = jnp.zeros((), BF)
+    one = jnp.ones((), BF)
+    row2 = lax.broadcasted_iota(jnp.int32, (256, 128), 0)
+    col2 = lax.broadcasted_iota(jnp.int32, (256, 128), 1)
+    swap = jnp.where(((row2 // 64) % 2) != (col2 // 64), 1.0, 0.0).astype(BF)
+
+    def fetch(head, h):
+        copies = []
+        for b in range(seq // block):
+            sl = pl.ds(b * block, block)
+            copies.append(
+                pltpu.make_async_copy(e_hbm.at[head, sl, :], ebuf.at[h, sl, :], esem.at[h, b])
+            )
+        return copies
+
+    for cp in fetch(0, 0):
+        cp.start()
+
+    def pair(p, carry):
+        cols = pl.ds(pl.multiple_of(p * 128, 128), 128)
+        qp, kp, vp, dop = q[:, cols], k[:, cols], v[:, cols], do[:, cols]
+        product = dop.astype(F32) * (o[:, cols].astype(F32) + ol[:, cols].astype(F32))
+        high = product.astype(BF)
+        rest = (product - high.astype(F32)).astype(BF)
+        inner = -dg(jnp.concatenate([high, rest], axis=1), swap)
+        inner_high = inner.astype(BF)
+        inner_rest = (inner - inner_high.astype(F32)).astype(BF)
+        do_t, q_t = dop.T, qp.T
+        dq_sum = None
+        dks, dvs = [], []
+        for h in range(2):
+            head = 2 * p + h
+
+            @pl.when(head + 1 < heads)
+            def unused_fetch():
+                for cp in fetch(head + 1, 1 - h):
+                    cp.start()
+
+            if h == 0:
+                lhs = jnp.where(low, dop, jnp.where(lane == 64, inner_high, inner_rest))
+                va = jnp.where(low, vp, jnp.where(lane < 66, one, zero))
+                km = jnp.where(low, kp, zero)
+            else:
+                lhs = jnp.where(low, jnp.where(lane == 0, inner_high, inner_rest), dop)
+                va = jnp.where(low, jnp.where(lane < 2, one, zero), vp)
+                km = jnp.where(low, zero, kp)
+            for cp in fetch(head, h):
+                cp.wait()
+            for b in range(seq // block):
+                sl = pl.ds(b * block, block)
+                t = dg(lhs[b * block : (b + 1) * block], va, NT)
+                ds[h, sl, :] = ebuf[h, sl, :] * t.astype(BF)
+            part = dg(ds[h], km)
+            dq_sum = part if dq_sum is None else dq_sum + part
+            dks.append(dg(q_t[64 * h : 64 * h + 64], ds[h]))
+            dvs.append(dg(do_t[64 * h : 64 * h + 64], ebuf[h]))
+        dq[:, cols] = (dq_sum * HD**-0.5).astype(BF)
+        dk[:, cols] = (jnp.concatenate(dks, axis=0) * LN2).astype(BF).T
+        dv[:, cols] = jnp.concatenate(dvs, axis=0).astype(BF).T
+        return carry
+
+    lax.fori_loop(0, heads // 2, pair, 0)
+
+
+def enc_forward(
+    len_ref, gains, shifts, x_hbm, w_hbm,
+    a0_o, q0_o, k0_o, v0_o, o0_o, ol0_o, r0_o, e0_o, x1_o, a1_o, h1_o, gp1_o, x2_o, mem_o,
+    x, wq, wk, wv, wo, wu, wd, a0, q, k, v, o, ol, r, x1, a1, h, gp, x2, mem, ebuf,
+    xsem, wsem, esem, osem,
+):
+    n1, n2 = wq.shape[1] // 2, wu.shape[1] // 2
+    cx = pltpu.make_async_copy(x_hbm, x, xsem.at[0])
+    cx.start()
+    loads = []
+    offset = 0
+    for i, (w, n) in enumerate(((wq, n1), (wk, n1), (wv, n1), (wo, n1), (wu, n2), (wd, n2))):
+        loads.append(load_weight(w_hbm, offset, n, w, wsem, 2 * i))
+        offset += n
+    cx.wait()
+    for i in range(3):
+        wait_all(loads[i])
+    saved = []
+
+    def save(src, dst):
+        cp = pltpu.make_async_copy(src, dst, osem.at[len(saved)])
+        cp.start()
+        saved.append(cp)
+
+    attn_project(x, gains[0:1, :], shifts[0:1, :], None, wq, wk, wv, a0, q, k, v)
+    save(a0, a0_o)
+    save(q, q0_o)
+    save(k, k0_o)
+    save(v, v0_o)
+    attn_core(len_ref[0], q, k, v, o, ol, r, e0_o, ebuf, esem)
+    save(o, o0_o)
+    save(ol, ol0_o)
+    save(r, r0_o)
+    wait_all(loads[3])
+    attn_join(x, o, wo, x1)
+    save(x1, x1_o)
+    wait_all(loads[4])
+    wait_all(loads[5])
+
+    def run(sl):
+        stream = x1[sl, :]
+        hat, unused = ln_hat(stream)
+        rows = (hat * gains[1:2, :] + shifts[1:2, :]).astype(BF)
+        a1[sl, :] = rows
+        active, slope = gelu_both(dg(rows, wu[...]))
+        active = active.astype(BF)
+        h[sl, :] = active
+        gp[sl, :] = slope.astype(BF)
+        out = stream + dg(active, wd[...], NT)
+        x2[sl, :] = out
+        hat, unused = ln_hat(out)
+        mem[sl, :] = (hat * gains[2:3, :] + shifts[2:3, :]).astype(BF)
+
+    rows_loop(x.shape[0], RB, run)
+    save(a1, a1_o)
+    save(h, h1_o)
+    save(gp, gp1_o)
+    save(x2, x2_o)
+    save(mem, mem_o)
+    wait_all(saved)
+
+
+def attn_backward(
+    g, x, gain, ng, index, a_t, kv_t, g_t, wq, wk, wv, wo, q, k, v, o, ol, r, e_hbm, ebuf, esem, ds,
+    do, dq, dk, dv, stage, slot, free, emit, into_keys, finish,
+):
+    seq = x.shape[0]
+
+    def before(sl):
+        rows = g[sl, :].astype(BF)
+        g_t[:, sl] = rows.T
+        do[sl, :] = (dg(rows, wo[...]) * r[sl, :].astype(F32)).astype(BF)
+
+    rows_loop(seq, RB, before)
+    free(slot + 3)
+    stage[slot + 3] = dg(g_t[...], o[...]).astype(BF)
+    emit(slot + 3)
+    attn_back_core(q, k, v, do, o, ol, e_hbm, ebuf, esem, ds, dq, dk, dv)
+    free(slot)
+    stage[slot] = dg(a_t[...], dq[...]).astype(BF)
+    emit(slot)
+    free(slot + 1)
+    stage[slot + 1] = dg(kv_t[...], dk[...]).astype(BF)
+    emit(slot + 1)
+    free(slot + 2)
+    stage[slot + 2] = dg(kv_t[...], dv[...]).astype(BF)
+    emit(slot + 2)
+
+    def after(sl):
+        into = dg(dq[sl, :], wq[...], NT)
+        keys = dg(dk[sl, :], wk[...], NT) + dg(dv[sl, :], wv[...], NT)
+        if into_keys is None:
+            into = into + keys
+        else:
+            into_keys[sl, :] = keys
+        dx, dgain, dshift = ln_back(x[sl, :].astype(F32), gain, into)
+        ng[index : index + 1, :] += dgain
+        ng[8 + index : 9 + index, :] += dshift
+        finish(sl, g[sl, :] + dx)
+
+    rows_loop(seq, RB, after)
+
+
+def dec_both(
+    len_ref, gains, shifts, y0_hbm, g3_hbm, mem_hbm, w_hbm,
+    dec_o, gy_o, ge_o, grad_o, ng, e3_o, e4_o,
+    y0, g3, mem, sq, sk, sv, so, cq, ck, cv, co, wu, wd, a3, q3, k3, v3, o3, ol3, r3, y1, a4, q4, k4, v4,
+    o4, ol4, r4, y2, a5, big, gs, do, a_t, kv_t, g_t, dec, stage, ebuf,
+    xsem, wsem, esem, osem,
+):
+    seq, width = y0.shape
+    n1, n2 = sq.shape[1] // 2, wu.shape[1] // 2
+    ins = []
+    for i, (src, dst) in enumerate(((y0_hbm, y0), (mem_hbm, mem), (g3_hbm, g3))):
+        cp = pltpu.make_async_copy(src, dst, xsem.at[i])
+        cp.start()
+        ins.append(cp)
+    loads = []
+    start = 4 * n1 + 2 * n2
+    offset = start
+    for i, (w, n) in enumerate(
+        ((sq, n1), (sk, n1), (sv, n1), (so, n1), (cq, n1), (ck, n1), (cv, n1), (co, n1), (wu, n2), (wd, n2))
+    ):
+        loads.append(load_weight(w_hbm, offset, n, w, wsem, 2 * i))
+        offset += n
+    ng[...] = jnp.zeros_like(ng)
+    ins[0].wait()
+    for i in range(3):
+        wait_all(loads[i])
+    attn_project(y0, gains[3:4, :], shifts[3:4, :], None, sq, sk, sv, a3, q3, k3, v3)
+    attn_core(seq, q3, k3, v3, o3, ol3, r3, e3_o, ebuf, esem)
+    wait_all(loads[3])
+    attn_join(y0, o3, so, y1)
+    ins[1].wait()
+    for i in range(4, 7):
+        wait_all(loads[i])
+    attn_project(y1, gains[4:5, :], shifts[4:5, :], mem, cq, ck, cv, a4, q4, k4, v4)
+    attn_core(len_ref[0], q4, k4, v4, o4, ol4, r4, e4_o, ebuf, esem)
+    wait_all(loads[7])
+    attn_join(y1, o4, co, y2)
+    ins[2].wait()
+    wait_all(loads[8])
+    wait_all(loads[9])
+    save = Saver(osem)
+    h, du = big.at[0], big.at[1]
+
+    def feed(sl):
+        stream = y2[sl, :]
+        hat, unused = ln_hat(stream)
+        rows = (hat * gains[5:6, :] + shifts[5:6, :]).astype(BF)
+        a_t[:, sl] = rows.T
+        active, slope = gelu_both(dg(rows, wu[...]))
+        active = active.astype(BF)
+        h[sl, :] = active
+        dec[sl, :] = (stream + dg(active, wd[...], NT)).astype(BF)
+        grad = g3[sl, :]
+        g_t[:, sl] = grad.T
+        lifted = (dg(grad, wd[...]) * slope).astype(BF)
+        du[sl, :] = lifted
+        into = dg(lifted, wu[...], NT)
+        dx, dgain, dshift = ln_back(stream, gains[5:6, :], into)
+        ng[5:6, :] += dgain
+        ng[13:14, :] += dshift
+        gs[sl, :] = grad.astype(F32) + dx
+
+    rows_loop(seq, RB, feed)
+    save(dec, dec_o, "dec")
+    parts = 2 * n2 // width
+
+    def emit_part(src_slot, offset, n, lower):
+        done = 0
+        while done < width:
+            t = (lower + done) // n
+            at = (lower + done) % n
+            take = min(width - done, n - at)
+            save(
+                stage.at[src_slot, :, pl.ds(done, take)],
+                grad_o.at[t, :, pl.ds(offset + at, take)],
+                src_slot,
+            )
+            done += take
+
+    ff_offset = 8 * n1
+    for j in range(parts):
+        cols = pl.ds(j * width, width)
+        stage[j] = dg(a_t[...], du[:, cols]).astype(BF)
+        emit_part(j, ff_offset, n2, j * width)
+        stage[parts + j] = dg(g_t[...], h[:, cols]).astype(BF)
+        emit_part(parts + j, ff_offset + n2, n2, j * width)
+
+    def emit(slot):
+        emit_part(slot, slot * n1, n1, 0)
+
+    ds = big.at[0]
+    ds_view = big.at[0]
+    dq, dk, dv = (big.at[1, :, pl.ds(i * width, width)] for i in range(3))
+    a_t[...] = a4[...].T
+    kv_t[...] = mem[...].T
+
+    def keep(sl, gradient):
+        gs[sl, :] = gradient
+
+    attn_backward(
+        gs, y1, gains[4:5, :], ng, 4, a_t, kv_t, g_t, cq, ck, cv, co, q4, k4, v4, o4, ol4, r4, e4_o,
+        ebuf, esem, SplitColumns(ds_view, seq), do, dq, dk, dv, stage, 4, save.free, emit, y2, keep,
+    )
+    save(y2, ge_o)
+    a_t[...] = a3[...].T
+
+    def last(sl, gradient):
+        dec[sl, :] = gradient.astype(BF)
+
+    save.free("dec")
+    attn_backward(
+        gs, y0, gains[3:4, :], ng, 3, a_t, a_t, g_t, sq, sk, sv, so, q3, k3, v3, o3, ol3, r3, e3_o,
+        ebuf, esem, SplitColumns(ds_view, seq), do, dq, dk, dv, stage, 0, save.free, emit, None, last,
+    )
+    save(dec, gy_o)
+    save.finish()
+
+
+class Saver:
+    def __init__(self, sems):
+        self.sems, self.count, self.live = sems, 0, []
+
+    def __call__(self, src, dst, slot=None):
+        cp = pltpu.make_async_copy(src, dst, self.sems.at[self.count])
+        cp.start()
+        self.count += 1
+        self.live.append((slot, cp))
+
+    def free(self, slot):
+        for name, cp in self.live:
+            if name == slot:
+                cp.wait()
+        self.live = [entry for entry in self.live if entry[0] != slot]
+
+    def finish(self):
+        for name, cp in self.live:
+            cp.wait()
+        self.live = []
+
+
+class SplitColumns:
+    def __init__(self, ref, n):
+        self.ref, self.n = ref, n
+
+    def cols(self, h):
+        return pl.ds(h * self.n, self.n)
+
+    def __getitem__(self, h):
+        return self.ref[:, self.cols(h)]
+
+    def __setitem__(self, key, value):
+        h, sl, unused = key
+        self.ref[sl, self.cols(h)] = value
+
+
+def enc_backward(
+    gains, shifts, ge_hbm, x_hbm, x1_hbm, x2_hbm, a0_hbm, q0_hbm, k0_hbm, v0_hbm, o0_hbm, ol0_hbm, r0_hbm,
+    a1_hbm, h1_hbm, gp1_hbm, e0_hbm, w_hbm,
+    sg_o, grad_o, ng,
+    ge, x, x1, x2, a0, q, k, v, o, ol, r, a1, big, wq, wk, wv, wo, wu, wd, gs, do, a_t, g_t, sg, stage, ebuf,
+    xsem, wsem, esem, osem,
+):
+    seq, width = x.shape
+    n1, n2 = wq.shape[1] // 2, wu.shape[1] // 2
+    ins = {}
+    order = (
+        ("ge", ge_hbm, ge), ("x2", x2_hbm, x2), ("gp", gp1_hbm, big.at[1]), ("x1", x1_hbm, x1),
+        ("a1", a1_hbm, a1), ("h", h1_hbm, big.at[0]), ("o", o0_hbm, o), ("ol", ol0_hbm, ol), ("r", r0_hbm, r),
+        ("q", q0_hbm, q), ("k", k0_hbm, k), ("v", v0_hbm, v), ("a0", a0_hbm, a0), ("x", x_hbm, x),
+    )
+    loads = {}
+
+    def begin(names):
+        for i, (name, src, dst) in enumerate(order):
+            if name in names:
+                cp = pltpu.make_async_copy(src, dst, xsem.at[i])
+                cp.start()
+                ins[name] = cp
+
+    begin(("ge", "x2", "gp", "x1"))
+    offsets = (0, n1, 2 * n1, 3 * n1, 4 * n1, 4 * n1 + n2)
+    for i, w in ((5, wd), (4, wu)):
+        loads[i] = load_weight(w_hbm, offsets[i], n2, w, wsem, 2 * i)
+    begin(("a1", "h", "o", "ol", "r", "q", "k", "v", "a0", "x"))
+    for i, w in ((3, wo), (0, wq), (1, wk), (2, wv)):
+        loads[i] = load_weight(w_hbm, offsets[i], n1, w, wsem, 2 * i)
+    ng[...] = jnp.zeros_like(ng)
+    for name in ("ge", "x2", "gp", "x1"):
+        ins[name].wait()
+    wait_all(loads[5])
+    wait_all(loads[4])
+    h, du = big.at[0], big.at[1]
+    save = Saver(osem)
+
+    def feed(sl):
+        dx, dgain, dshift = ln_back(x2[sl, :], gains[2:3, :], ge[sl, :])
+        ng[2:3, :] += dgain
+        ng[10:11, :] += dshift
+        grad = dx.astype(BF)
+        g_t[:, sl] = grad.T
+        lifted = (dg(grad, wd[...]) * du[sl, :].astype(F32)).astype(BF)
+        du[sl, :] = lifted
+        into = dg(lifted, wu[...], NT)
+        dx1, dgain, dshift = ln_back(x1[sl, :], gains[1:2, :], into)
+        ng[1:2, :] += dgain
+        ng[9:10, :] += dshift
+        gs[sl, :] = dx + dx1
+
+    rows_loop(seq, RB, feed)
+    parts = 2 * n2 // width
+
+    def emit_part(src_slot, offset, n, lower):
+        done = 0
+        while done < width:
+            t = (lower + done) // n
+            at = (lower + done) % n
+            take = min(width - done, n - at)
+            save(
+                stage.at[src_slot, :, pl.ds(done, take)],
+                grad_o.at[t, :, pl.ds(offset + at, take)],
+            )
+            done += take
+
+    ins["a1"].wait()
+    ins["h"].wait()
+    a_t[...] = a1[...].T
+    for j in range(parts):
+        cols = pl.ds(j * width, width)
+        stage[4 + j] = dg(a_t[...], du[:, cols]).astype(BF)
+        emit_part(4 + j, 4 * n1, n2, j * width)
+        stage[4 + parts + j] = dg(g_t[...], h[:, cols]).astype(BF)
+        emit_part(4 + parts + j, 4 * n1 + n2, n2, j * width)
+    for name in ("o", "ol", "r", "q", "k", "v", "a0", "x"):
+        ins[name].wait()
+    for i in range(4):
+        wait_all(loads[i])
+    a_t[...] = a0[...].T
+
+    def emit(slot):
+        emit_part(slot, slot * n1, n1, 0)
+
+    def last(sl, gradient):
+        sg[sl, :] = gradient.astype(BF)
+
+    dq, dk, dv = (big.at[1, :, pl.ds(i * width, width)] for i in range(3))
+    attn_backward(
+        gs, x, gains[0:1, :], ng, 0, a_t, a_t, g_t, wq, wk, wv, wo, q, k, v, o, ol, r, e0_hbm,
+        ebuf, esem, SplitColumns(big.at[0], seq), do, dq, dk, dv, stage, 0, save.free, emit, None, last,
+    )
+    save(sg, sg_o)
+    save.finish()
+
+
+def compute_all(length, gains, shifts, x, y0, g3, weights):
+    seq, width = x.shape
+    total = weights.shape[2]
+    n1 = width // 2
+    n2 = (total - 12 * n1) // 4
+    hidden = 2 * n2
+    heads = width // HD
+    sd = jax.ShapeDtypeStruct
+    any_spec = pl.BlockSpec(memory_space=pl.ANY)
+    vmem = pl.BlockSpec(memory_space=pltpu.VMEM)
+    smem = pl.BlockSpec(memory_space=pltpu.SMEM)
+    dma = pltpu.SemaphoreType.DMA
+    row = lambda kind: sd((seq, width), kind)
+    tall = lambda kind: sd((seq, hidden), kind)
+    escores = sd((heads, seq, seq), BF)
+    vrow = lambda kind: pltpu.VMEM((seq, width), kind)
+    vsq = pltpu.VMEM((width, width), BF)
+    vwide = pltpu.VMEM((width, hidden), BF)
+    vtall = pltpu.VMEM((seq, hidden), BF)
+    params = pltpu.CompilerParams(vmem_limit_bytes=VMEM_LIMIT)
+    (a0, q0, k0, v0, o0, ol0, r0, e0, x1, a1, h1, gp1, x2, mem) = pl.pallas_call(
+        enc_forward,
+        in_specs=[smem, vmem, vmem, any_spec, any_spec],
+        out_specs=[any_spec] * 14,
+        out_shape=[row(BF)] * 7 + [escores, row(F32), row(BF), tall(BF), tall(BF), row(F32), row(BF)],
+        scratch_shapes=[vrow(BF)] + [vsq] * 4 + [vwide] * 2 + [vrow(BF)] * 7
+        + [vrow(F32), vrow(BF), vtall, vtall, vrow(F32), vrow(BF), pltpu.VMEM((2, seq, seq), BF)]
+        + [dma((1,)), dma((12,)), dma((2, 2)), dma((13,))],
+        compiler_params=params,
+        name="enc_forward",
+    )(length, gains, shifts, x, weights)
+    slots = max(8, 2 * (hidden // width))
+    dec, gy, ge, gdec, ng_dec, unused3, unused4 = pl.pallas_call(
+        dec_both,
+        in_specs=[smem, vmem, vmem] + [any_spec] * 4,
+        out_specs=[any_spec] * 4 + [vmem, any_spec, any_spec],
+        out_shape=[row(BF), row(BF), row(F32), sd((2, width, 8 * n1 + 2 * n2), BF), sd((16, width), F32)]
+        + [escores] * 2,
+        scratch_shapes=[vrow(BF)] * 3 + [vsq] * 8 + [vwide] * 2 + [vrow(BF)] * 7 + [vrow(F32)]
+        + [vrow(BF)] * 7 + [vrow(F32), vrow(BF), pltpu.VMEM((2, seq, hidden), BF), vrow(F32), vrow(BF)]
+        + [pltpu.VMEM((width, seq), BF)] * 3 + [vrow(BF), pltpu.VMEM((slots, width, width), BF)]
+        + [pltpu.VMEM((2, seq, seq), BF)]
+        + [dma((3,)), dma((20,)), dma((2, 2)), dma((3 + 4 * slots,))],
+        compiler_params=params,
+        name="dec_both",
+    )(length, gains, shifts, y0, g3, mem, weights)
+    slots = 4 + 2 * (hidden // width)
+    sg, genc, ng_enc = pl.pallas_call(
+        enc_backward,
+        in_specs=[vmem, vmem] + [any_spec] * 16,
+        out_specs=[any_spec] * 2 + [vmem],
+        out_shape=[row(BF), sd((2, width, 4 * n1 + 2 * n2), BF), sd((16, width), F32)],
+        scratch_shapes=[vrow(F32), vrow(BF), vrow(F32), vrow(F32)] + [vrow(BF)] * 8
+        + [pltpu.VMEM((2, seq, hidden), BF)] + [vsq] * 4 + [vwide] * 2 + [vrow(F32), vrow(BF)]
+        + [pltpu.VMEM((width, seq), BF)] * 2 + [vrow(BF), pltpu.VMEM((slots, width, width), BF)]
+        + [pltpu.VMEM((2, seq, seq), BF)]
+        + [dma((14,)), dma((12,)), dma((2, 2)), dma((3 + 4 * slots,))],
+        compiler_params=params,
+        name="enc_backward",
+    )(gains, shifts, ge, x, x1, x2, a0, q0, k0, v0, o0, ol0, r0, a1, h1, gp1, e0, weights)
+    return dec, sg, gy, genc, gdec, ng_enc + ng_dec
+
+
+def places():
+    d = lax.axis_index("dp")
+    return lax.axis_index("tensor"), d // 4, (d // 2) % 2, d % 2
+
+
+def at(t, z, y, c):
+    return (z * 4 + y * 2 + c, t)
+
+
+def greet(partners):
+    barrier = pltpu.get_barrier_semaphore()
+    for device in partners:
+        pl.semaphore_signal(barrier, inc=1, device_id=device, device_id_type=MESH)
+    pl.semaphore_wait(barrier, len(partners))
+
+
+def all_partners(t, z, y, c):
+    others = [at(t, lax.rem(z + j, 4), y, c) for j in range(1, 4)]
+    return [at(t, z, y, 1 - c), at(1 - t, z, y, c), at(t, z, 1 - y, c)] + others
+
+
+CHUNK = 1024
+
+
+def gather_weights(own, out, send, recv, local):
+    t, z, y, c = places()
+    greet(all_partners(t, z, y, c))
+    cp = pltpu.make_async_copy(own, out.at[t, z, y, c], local.at[0])
+    cp.start()
+    chunks = own.shape[1] // CHUNK
+    half = CHUNK // 2
+    sends = []
+
+    def push(src, dst, k, i, device):
+        copy = pltpu.make_async_remote_copy(
+            src_ref=src, dst_ref=dst, send_sem=send.at[k, i], recv_sem=recv.at[k, i],
+            device_id=device, device_id_type=MESH,
+        )
+        copy.start()
+        sends.append(copy)
+        return copy
+
+    pending = {}
+
+    def stage(k, s):
+        full = pl.ds(k * CHUNK, CHUNK)
+        left = pl.ds(k * CHUNK, half)
+        right = pl.ds(k * CHUNK + half, half)
+        if s == 0:
+            pending[k] = [
+                push(own.at[:, full], out.at[t, z, y, c, :, full], k, j - 1, at(t, lax.rem(z + j, 4), y, c))
+                for j in range(1, 4)
+            ]
+            return
+        for copy in pending[k]:
+            copy.wait_recv()
+        if s == 1:
+            a = out.at[t, :, y, c, :, left]
+            b = out.at[t, :, y, c, :, right]
+            pending[k] = [push(a, a, k, 3, at(1 - t, z, y, c)), push(b, b, k, 4, at(t, z, 1 - y, c))]
+        elif s == 2:
+            a = out.at[:, :, y, c, :, left]
+            b = out.at[t, :, :, c, :, right]
+            pending[k] = [push(a, a, k, 5, at(t, z, 1 - y, c)), push(b, b, k, 6, at(1 - t, z, y, c))]
+        elif s == 3:
+            a = out.at[:, :, :, c, :, full]
+            pending[k] = [push(a, a, k, 7, at(t, z, y, 1 - c))]
+
+    for tick in range(chunks + 4):
+        if tick == 1:
+            cp.wait()
+        for s in (4, 3, 2, 1, 0):
+            k = tick - s
+            if 0 <= k < chunks:
+                stage(k, s)
+    for copy in sends:
+        copy.wait_send()
+
+
+def sum_grads(genc, gdec, vec, out, vec_out, r1, s1, r2a, r2b, s2a, s2b, r3a, r3b, s3, r4, v1, vr, send, recv, local, vsend, vrecv):
+    t, z, y, c = places()
+    greet(all_partners(t, z, y, c))
+    enc_chunks = genc.shape[-1] // CHUNK
+    chunks = enc_chunks + gdec.shape[-1] // CHUNK
+    half = CHUNK // 2
+    sends = []
+
+    def push(src, dst, ssem, rsem, device):
+        copy = pltpu.make_async_remote_copy(
+            src_ref=src, dst_ref=dst, send_sem=ssem, recv_sem=rsem, device_id=device, device_id_type=MESH,
+        )
+        copy.start()
+        sends.append(copy)
+        return copy
+
+    def big(k):
+        if k < enc_chunks:
+            return genc, pl.ds(k * CHUNK, CHUNK)
+        return gdec, pl.ds((k - enc_chunks) * CHUNK, CHUNK)
+
+    pending, own = {}, {}
+    left, right = pl.ds(0, half), pl.ds(half, half)
+
+    def stage(k, s):
+        if s == 0:
+            g, cols = big(k)
+            own[k] = pltpu.make_async_copy(g.at[:, :, :, c, :, cols], s1.at[k], local.at[k])
+            own[k].start()
+            pending[k] = [push(g.at[:, :, :, 1 - c, :, cols], r1.at[k], send.at[k, 0], recv.at[k, 0], at(t, z, y, 1 - c))]
+            return
+        for copy in pending[k]:
+            copy.wait_recv()
+        if s == 1:
+            own[k].wait()
+            s1[k] = (s1[k].astype(F32) + r1[k].astype(F32)).astype(BF)
+            pending[k] = [
+                push(s1.at[k, 1 - t, :, :, :, left], r2a.at[k], send.at[k, 1], recv.at[k, 1], at(1 - t, z, y, c)),
+                push(s1.at[k, :, :, 1 - y, :, right], r2b.at[k], send.at[k, 2], recv.at[k, 2], at(t, z, 1 - y, c)),
+            ]
+        elif s == 2:
+            s2a[k] = (s1[k, t, :, :, :, left].astype(F32) + r2a[k].astype(F32)).astype(BF)
+            s2b[k] = (s1[k, :, :, y, :, right].astype(F32) + r2b[k].astype(F32)).astype(BF)
+            pending[k] = [
+                push(s2a.at[k, :, 1 - y], r3a.at[k], send.at[k, 3], recv.at[k, 3], at(t, z, 1 - y, c)),
+                push(s2b.at[k, 1 - t], r3b.at[k], send.at[k, 4], recv.at[k, 4], at(1 - t, z, y, c)),
+            ]
+        elif s == 3:
+            s3[k, :, :, left] = (s2a[k, :, y].astype(F32) + r3a[k].astype(F32)).astype(BF)
+            s3[k, :, :, right] = (s2b[k, t].astype(F32) + r3b[k].astype(F32)).astype(BF)
+            pending[k] = []
+            for j in range(1, 4):
+                zz = lax.rem(z + j, 4)
+                pending[k].append(push(s3.at[k, zz], r4.at[k, j - 1], send.at[k, 4 + j], recv.at[k, 4 + j], at(t, zz, y, c)))
+        elif s == 4:
+            out[:, pl.ds(k * CHUNK, CHUNK)] = (s3[k, z].astype(F32) + r4[k, 0].astype(F32)) + (
+                r4[k, 1].astype(F32) + r4[k, 2].astype(F32)
+            )
+
+    vpending = []
+
+    def vector_stage(s):
+        for copy in vpending:
+            copy.wait_recv()
+        vpending.clear()
+        if s == 0:
+            v1[0] = vec[...]
+        elif s < 4:
+            v1[s] = v1[s - 1] + vr[s - 1]
+        if s < 3:
+            device = (at(t, z, y, 1 - c), at(1 - t, z, y, c), at(t, z, 1 - y, c))[s]
+            vpending.append(push(v1.at[s], vr.at[s], vsend.at[s], vrecv.at[s], device))
+        elif s == 3:
+            for j in range(1, 4):
+                vpending.append(
+                    push(v1.at[3], vr.at[2 + j], vsend.at[2 + j], vrecv.at[2 + j], at(t, lax.rem(z + j, 4), y, c))
+                )
+        else:
+            vec_out[...] = (v1[3] + vr[3]) + (vr[4] + vr[5])
+
+    for tick in range(chunks + 4):
+        for s in (4, 3, 2, 1, 0):
+            k = tick - s
+            if 0 <= k < chunks:
+                stage(k, s)
+        if tick < 5:
+            vector_stage(tick)
+    for copy in sends:
+        copy.wait_send()
+
+
+def call_gather(own):
+    rows, n = own.shape
+    chunks = n // CHUNK
+    any_spec = pl.BlockSpec(memory_space=pl.ANY)
+    dma = pltpu.SemaphoreType.DMA
+    return pl.pallas_call(
+        gather_weights,
+        in_specs=[any_spec],
+        out_specs=any_spec,
+        out_shape=jax.ShapeDtypeStruct((2, 4, 2, 2, rows, n), BF),
+        scratch_shapes=[dma((chunks, 8)), dma((chunks, 8)), dma((1,))],
+        compiler_params=pltpu.CompilerParams(collective_id=0, has_side_effects=True),
+        name="gather_weights",
+    )(own)
+
+
+def call_sum(genc, gdec, vec):
+    rows = genc.shape[1] // 16
+    split = lambda g: g.reshape(2, 4, 2, 2, rows, g.shape[2])
+    n = genc.shape[2] + gdec.shape[2]
+    chunks = n // CHUNK
+    half = CHUNK // 2
+    any_spec = pl.BlockSpec(memory_space=pl.ANY)
+    vmem = pl.BlockSpec(memory_space=pltpu.VMEM)
+    dma = pltpu.SemaphoreType.DMA
+    buf = lambda *dims: pltpu.VMEM((chunks,) + dims, BF)
+    return pl.pallas_call(
+        sum_grads,
+        in_specs=[any_spec, any_spec, vmem],
+        out_specs=[vmem, vmem],
+        out_shape=[jax.ShapeDtypeStruct((rows, n), F32), jax.ShapeDtypeStruct(vec.shape, F32)],
+        scratch_shapes=[
+            buf(2, 4, 2, rows, CHUNK), buf(2, 4, 2, rows, CHUNK),
+            buf(4, 2, rows, half), buf(2, 4, rows, half), buf(4, 2, rows, half), buf(2, 4, rows, half),
+            buf(4, rows, half), buf(4, rows, half), buf(4, rows, CHUNK), buf(3, rows, CHUNK),
+            pltpu.VMEM((4,) + vec.shape, F32), pltpu.VMEM((6,) + vec.shape, F32),
+            dma((chunks, 8)), dma((chunks, 8)), dma((chunks,)), dma((6,)), dma((6,)),
+        ],
+        compiler_params=pltpu.CompilerParams(
+            collective_id=1, has_side_effects=True, vmem_limit_bytes=VMEM_LIMIT
+        ),
+        name="sum_grads",
+    )(split(genc), split(gdec), vec)
+
+
+def swap_halves(arrays):
+    t = lax.axis_index("tensor")
+    results = []
+    for mine in arrays:
+        sent = lax.dynamic_index_in_dim(mine, 1 - t, 0, keepdims=False)
+        kept = lax.dynamic_index_in_dim(mine, t, 0, keepdims=False)
+        got = lax.ppermute(sent, "tensor", [(0, 1), (1, 0)])
+        low = jnp.where(t == 0, kept, got)
+        high = jnp.where(t == 0, got, kept)
+        results.append(jnp.concatenate([low, high], axis=0))
+    return results
+
+
+def return_halves(whole):
+    t = lax.axis_index("tensor")
+    rows = whole.shape[0] // 2
+    parts = whole.reshape(2, rows, whole.shape[1])
+    sent = lax.dynamic_index_in_dim(parts, 1 - t, 0, keepdims=False)
+    kept = lax.dynamic_index_in_dim(parts, t, 0, keepdims=False)
+    got = lax.ppermute(sent, "tensor", [(0, 1), (1, 0)])
+    return jnp.stack([jnp.where(t == 0, kept, got), jnp.where(t == 0, got, kept)])
+
+
+def pair_body(*arguments):
+    source, target, cotangent, lengths, timesteps, masked, loss_mask = arguments[:7]
+    matrices = arguments[7:23]
+    norm_gains, norm_shifts, mask_vector = arguments[23:]
+    t = lax.axis_index("tensor")
+    turned = (3, 5, 9, 13, 15)
+    own = jnp.concatenate([m.T if i in turned else m for i, m in enumerate(matrices)], axis=1)
+    gathered = call_gather(own)
+    weights = gathered.reshape(2, 16 * own.shape[0], own.shape[1])
+    chosen = masked[:, :, None] == 1
+    start_y = jnp.where(chosen, mask_vector, target.astype(F32)).astype(BF)
+    factor = (STEPS + 1 - timesteps).astype(F32) / STEPS
+    grad3 = (
+        cotangent.astype(F32) * (factor[:, None] * loss_mask.astype(F32))[:, :, None]
+    ).astype(BF)
+    x, y0, g3 = swap_halves((source, start_y, grad3))
+    length = lax.dynamic_slice_in_dim(lengths, t, 1)
+    dec, sg, gy, genc, gdec, ng = compute_all(length, norm_gains, norm_shifts, x, y0, g3, weights)
+    decoded = return_halves(dec)
+    grad_y = return_halves(gy)
+    target_grad = jnp.where(chosen, jnp.zeros((), BF), grad_y)
+    mask_part = jnp.sum(jnp.where(chosen, grad_y.astype(F32), 0.0), axis=(0, 1))
+    source_grad = return_halves(sg)
+    vec = jnp.concatenate([ng[:6], ng[8:14], mask_part[None], jnp.zeros((3, ng.shape[1]), F32)], axis=0)
+    summed, vec = call_sum(genc, gdec, vec)
+    grads, offset = [], 0
+    for i, m in enumerate(matrices):
+        n = m.shape[0] if i in turned else m.shape[1]
+        part = summed[:, offset : offset + n]
+        offset += n
+        grads.append(part.T if i in turned else part)
+    return (decoded, source_grad, target_grad, *grads, vec[:6], vec[6:12], vec[12])
+
+
 def solution(mesh):
+    whole_pairs = dict(mesh.shape) == {"dp": 16, "tensor": 2}
     return jax.shard_map(
-        body,
+        pair_body if whole_pairs else body,
         mesh=mesh,
         in_specs=(
             P("dp", "tensor", None),

time: 2430 us -> 470 us (0.19)
  waiting for transfers between devices: 1350 us -> 0.02 us
  matrix products: 532 us -> 0 us
  Pallas kernels: 0 us -> 413 us
  blocking collectives: 275 us -> 0 us
  other arithmetic: 194 us -> 16.4 us
    reduce_scatter x36 -> x0, waiting for transfers between devices: 1170 us -> none  [the longest x8 184 us: collect_grad(): lax.psum_scatter(partial_value, 'tensor', scatter_dimension=1, tiled=True)]
    dot_general x168 -> x0, matrix products: 532 us -> none  [the longest x32 98.8 us: project(): jnp.einsum('bsk,kn->bsn', inputs, weight, preferred_element_type=jnp.floa...]
    pallas_call x0 -> x5, Pallas kernels: none -> 413 us  [the longest x1 135 us: compute_all(): pl.pallas_call(dec_both, in_specs=[smem, vmem, vmem] + [any_spec] * 4, ou...]
    all_gather x12 -> x0, blocking collectives: 235 us -> none  [the longest x1 23.8 us: body(): lax.all_gather(enc_query, 'dp', axis=0, tiled=True)]
    all_gather x22 -> x0, waiting for transfers between devices: 168 us -> none  [the longest x6 53.5 us: spread_grad(): lax.all_gather(gradient.astype(jnp.bfloat16), 'tensor', axis=1, tiled=True)]
    convert_element_type x37 -> x2, other arithmetic: 111 us -> 1.83 us  [the longest x1 1.54 us: pair_body(): start_y = jnp.where(chosen, mask_vector, target.astype(F32)).astype(BF)]
    reduce_sum x42 -> x1, other arithmetic: 75.7 us -> 0.3 us  [pair_body(): mask_part = jnp.sum(jnp.where(chosen, grad_y.astype(F32), 0.0), axis=(0, 1))]
    psum x1 -> x0, blocking collectives: 40.4 us -> none  [body(): vectors = lax.psum((gain_total, shift_total, mask_total), ('dp', 'tensor'))]
  transfers between devices with their start and end apart: 60 -> 6, of which waited for: 37 -> 0; matrix products, arithmetic and copies ran while one was open for 27% -> 6% of each run, Pallas kernels for 0% -> 50%
where the time goes in v1:
time: 470 us; the launch traced here: 461 us
  Pallas kernels  413 us (88%)
  local copies, waits for them, and re-layouts  22.3 us (5%)
  other arithmetic  16.4 us (3%)
  starting transfers between devices  7.9 us (2%)
    pallas_call x1, Pallas kernels, compute_all(): pl.pallas_call(dec_both, in_specs=[smem, vmem, vmem] + [any_spec] * 4, ou...  135 us
    pallas_call x1, Pallas kernels, call_sum(): pl.pallas_call(sum_grads, in_specs=[any_spec, any_spec, vmem], out_specs=...  94.2 us
    pallas_call x1, Pallas kernels, call_gather(): pl.pallas_call(gather_weights, in_specs=[any_spec], out_specs=any_spec, o...  89.6 us
    pallas_call x1, Pallas kernels, compute_all(): pl.pallas_call(enc_backward, in_specs=[vmem, vmem] + [any_spec] * 16, out...  47.4 us
    pallas_call x1, Pallas kernels, compute_all(): pl.pallas_call(enc_forward, in_specs=[smem, vmem, vmem, any_spec, any_spe...  47.1 us
  transfers between devices with their start and end apart: 6, of which 0 were waited for; matrix products, arithmetic and copies ran while one was open for 6% of the time, Pallas kernels for 50%

profile of v1, /device:TPU:0, one launch (start us, length us, event | category | flops | bytes accessed | tf_op | source)
XLA Modules:
  0.0 461.1 jit_solution(13776372963643775979)
XLA Ops:
  0.7 0.8 broadcast_compare_fusion
  1.5 1.5 select_convert_fusion
  3.0 0.8 dynamic-slice_bitcast_fusion.5
  3.9 2.9 collective-permute-start
  7.4 0.8 dynamic-slice_bitcast_fusion.4
  8.2 0.8 dynamic-slice_bitcast_fusion.3
  9.0 2.0 collective-permute-start.2
  20.9 89.6 %gather_weights.1 = bf16[2,4,2,2,32,7168]{5,4,3,2,1,0:T(8,128)(2,1)} custom-call(bf16[32,7168]{1,0:T(8,128)(2,1)} %bitcast_dynamic-update-slice_fusion.own), custom_call_target="tpu_custom_call" | custom-call | tf_op jit(solution)/shard_map/gather_weights/pallas_call | solution.py:1270
  111.1 1.1 bitcast_select_fusion.7
  112.3 1.0 pad_maximum_fusion.2.x_hbm
  113.3 1.1 bitcast_select_fusion.11
  114.4 1.1 bitcast_select_fusion.9
  115.5 1.5 pad_maximum_fusion
  117.0 47.1 %enc_forward.1 = (bf16[1024,512]{1,0:T(8,128)(2,1)}, bf16[1024,512]{1,0:T(8,128)(2,1)}, bf16[1024,512]{1,0:T(8,128)(2,1)}, bf16[1024,512]{1,0:T(8,128)(2,1)}, bf...) custom-call(s32[1]{0:T(128)} %dynamic_slice.40.len_ref, ...), custom_call_target="tpu_custom_call" | custom-call | tf_op jit(solution)/shard_map/enc_forward/pallas_call | solution.py:1052
  164.1 134.9 %dec_both.1 = (bf16[1024,512]{1,0:T(8,128)(2,1)}, bf16[1024,512]{1,0:T(8,128)(2,1)}, f32[1024,512]{1,0:T(8,128)}, bf16[2,512,4096]{2,1,0:T(8,128)(2,1)}, f32[16,...) custom-call(s32[1]{0:T(128)} %dynamic_slice.40.len_ref, f32[6,512]{1,0:T(8,128)} %gains.5, ...), custom_call_target="tpu_custom_call" | custom-call | tf_op jit(solution)/shard_map/dec_both/pallas_call | solution.py:1064
  299.0 1.9 dynamic-slice_bitcast_fusion
  300.8 0.8 collective-permute-start.5
  301.8 47.4 %enc_backward.1 = (bf16[1024,512]{1,0:T(8,128)(2,1)}, bf16[2,512,3072]{2,1,0:T(8,128)(2,1)}, f32[16,512]{1,0:T(8,128)}) custom-call(f32[6,512]{1,0:T(8,128)} %gains.5, f32[6,512]{1,0:T(8,128)} %shifts.5, f32[1024,512]{1,0:T(8,128)} %get-tuple-element.48.ge_hbm, bf16[1024,512]{1,0:T(8,128)(2,1)} %pad_maximum_fusion.2.x_hbm, ...), custom_call_target="tpu_custom_call" | custom-call | tf_op jit(solution)/shard_map/enc_backward/pallas_call | solution.py:1079
  349.2 2.0 dynamic-slice_bitcast_fusion.1
  351.1 1.2 collective-permute-start.4
  352.4 0.9 collective-permute-start.3
  353.3 1.1 fusion
  355.4 94.2 %sum_grads.1 = (f32[32,7168]{1,0:T(8,128)}, f32[16,512]{1,0:T(8,128)}) custom-call(bf16[2,4,2,2,32,3072]{5,4,3,2,1,0:T(8,128)(2,1)} %bitcast.86, bf16[2,4,2,2,32,4096]{5,4,3,2,1,0:T(8,128)(2,1)} %bitcast.85, f32[16,512]{1,0:T(8,128)} %maximum_maximum_fusion.vec), custom_call_target="tpu_custom_call" | custom-call | tf_op jit(solution)/shard_map/sum_grads/pallas_call | solution.py:1291
  449.6 1.4 fusion.6
  451.0 1.7 slice_bitcast_fusion.2
  452.7 1.4 fusion.2
  454.1 1.1 pad_maximum_fusion.4
  455.2 1.4 slice.83
  456.5 0.8 slice_bitcast_fusion
  457.3 1.2 broadcast_select_fusion
  458.5 1.1 fusion.4
  459.6 1.1 pad_maximum_fusion.3
  (90 shorter events, 12.0 us)
Async XLA Ops:
  0.7 6.2 %copy-start.26 = (s32[2]{0:T(128)S(1)}, s32[2]{0:T(128)}, u32[]{:S(2)}) copy-start(s32[2]{0:T(128)} %param.30) | copy-start | bytes 28
  0.7 6.1 %copy-start.25 = (s32[2,512]{1,0:T(2,128)S(1)}, s32[2,512]{1,0:T(2,128)}, u32[]{:S(2)}) copy-start(s32[2,512]{1,0:T(2,128)} %param.32) | copy-start | bytes 12292
  0.7 6.2 %copy-start = (bf16[2,512,512]{2,1,0:T(8,128)(2,1)S(1)}, bf16[2,512,512]{2,1,0:T(8,128)(2,1)}, u32[]{:S(2)}) copy-start(bf16[2,512,512]{2,1,0:T(8,128)(2,1)} %param.28) | copy-start | bytes 3145732
  3.0 5.2 %copy-start.1 = (bf16[2,512,512]{2,1,0:T(8,128)(2,1)S(1)}, bf16[2,512,512]{2,1,0:T(8,128)(2,1)}, u32[]{:S(2)}) copy-start(bf16[2,512,512]{2,1,0:T(8,128)(2,1)} %param.26) | copy-start | bytes 3145732
  3.9 109.4 %collective-permute-start = (bf16[512,512]{1,0:T(8,128)(2,1)}, bf16[512,512]{1,0:T(8,128)(2,1)}, u32[]{:S(2)}, u32[]{:S(2)}) collective-permute-start(bf16[512,512]{1,0:T(8,128)(2,1)} %dynamic-slice_bitcast_fusion.5), channel_id=1, source_target_pairs={{0,1},{1,0},{2,3},{3,2},{4,5},{5,4},{6,7},{7,6},{8,9},{9,8},{10,11... | collective-permute-start | bytes 1572872 | tf_op jit(solution)/shard_map/ppermute | solution.py:1316
  6.9 4.2 copy-start.13
  6.9 4.8 %copy-start.14 = (bf16[32,256]{1,0:T(8,128)(2,1)S(1)}, bf16[32,256]{1,0:T(8,128)(2,1)}, u32[]{:S(2)}) copy-start(bf16[32,256]{1,0:T(8,128)(2,1)} %param.34) | copy-start | bytes 49156
  6.9 5.4 %copy-start.15 = (bf16[32,256]{1,0:T(8,128)(2,1)S(1)}, bf16[32,256]{1,0:T(8,128)(2,1)}, u32[]{:S(2)}) copy-start(bf16[32,256]{1,0:T(8,128)(2,1)} %param.35) | copy-start | bytes 49156
  6.9 6.0 %copy-start.16 = (bf16[256,32]{0,1:T(8,128)(2,1)S(1)}, bf16[256,32]{0,1:T(8,128)(2,1)}, u32[]{:S(2)}) copy-start(bf16[256,32]{0,1:T(8,128)(2,1)} %param.36) | copy-start | bytes 49156
  6.9 6.6 %copy-start.7 = (bf16[32,1024]{1,0:T(8,128)(2,1)S(1)}, bf16[32,1024]{1,0:T(8,128)(2,1)}, u32[]{:S(2)}) copy-start(bf16[32,1024]{1,0:T(8,128)(2,1)} %param.37) | copy-start | bytes 196612
  6.9 7.2 %copy-start.8 = (bf16[1024,32]{0,1:T(8,128)(2,1)S(1)}, bf16[1024,32]{0,1:T(8,128)(2,1)}, u32[]{:S(2)}) copy-start(bf16[1024,32]{0,1:T(8,128)(2,1)} %param.38) | copy-start | bytes 196612
  6.9 7.8 %copy-start.17 = (bf16[32,256]{1,0:T(8,128)(2,1)S(1)}, bf16[32,256]{1,0:T(8,128)(2,1)}, u32[]{:S(2)}) copy-start(bf16[32,256]{1,0:T(8,128)(2,1)} %param.39) | copy-start | bytes 49156
  7.0 8.4 %copy-start.18 = (bf16[32,256]{1,0:T(8,128)(2,1)S(1)}, bf16[32,256]{1,0:T(8,128)(2,1)}, u32[]{:S(2)}) copy-start(bf16[32,256]{1,0:T(8,128)(2,1)} %param.40) | copy-start | bytes 49156
  7.0 9.0 %copy-start.19 = (bf16[32,256]{1,0:T(8,128)(2,1)S(1)}, bf16[32,256]{1,0:T(8,128)(2,1)}, u32[]{:S(2)}) copy-start(bf16[32,256]{1,0:T(8,128)(2,1)} %param.41) | copy-start | bytes 49156
  7.0 9.6 %copy-start.20 = (bf16[256,32]{0,1:T(8,128)(2,1)S(1)}, bf16[256,32]{0,1:T(8,128)(2,1)}, u32[]{:S(2)}) copy-start(bf16[256,32]{0,1:T(8,128)(2,1)} %param.42) | copy-start | bytes 49156
  7.0 12.6 %copy-start.9 = (bf16[32,1024]{1,0:T(8,128)(2,1)S(1)}, bf16[32,1024]{1,0:T(8,128)(2,1)}, u32[]{:S(2)}) copy-start(bf16[32,1024]{1,0:T(8,128)(2,1)} %param.47) | copy-start | bytes 196612
  7.0 13.3 %copy-start.10 = (bf16[1024,32]{0,1:T(8,128)(2,1)S(1)}, bf16[1024,32]{0,1:T(8,128)(2,1)}, u32[]{:S(2)}) copy-start(bf16[1024,32]{0,1:T(8,128)(2,1)} %param.48) | copy-start | bytes 196612
  7.3 9.9 %copy-start.21 = (bf16[32,256]{1,0:T(8,128)(2,1)S(1)}, bf16[32,256]{1,0:T(8,128)(2,1)}, u32[]{:S(2)}) copy-start(bf16[32,256]{1,0:T(8,128)(2,1)} %param.43) | copy-start | bytes 49156
  7.3 10.5 %copy-start.22 = (bf16[32,256]{1,0:T(8,128)(2,1)S(1)}, bf16[32,256]{1,0:T(8,128)(2,1)}, u32[]{:S(2)}) copy-start(bf16[32,256]{1,0:T(8,128)(2,1)} %param.44) | copy-start | bytes 49156
  7.3 11.1 %copy-start.23 = (bf16[32,256]{1,0:T(8,128)(2,1)S(1)}, bf16[32,256]{1,0:T(8,128)(2,1)}, u32[]{:S(2)}) copy-start(bf16[32,256]{1,0:T(8,128)(2,1)} %param.45) | copy-start | bytes 49156
  7.3 11.7 %copy-start.24 = (bf16[256,32]{0,1:T(8,128)(2,1)S(1)}, bf16[256,32]{0,1:T(8,128)(2,1)}, u32[]{:S(2)}) copy-start(bf16[256,32]{0,1:T(8,128)(2,1)} %param.46) | copy-start | bytes 49156
  8.2 106.2 %collective-permute-start.1 = (bf16[512,512]{1,0:T(8,128)(2,1)}, bf16[512,512]{1,0:T(8,128)(2,1)}, u32[]{:S(2)}, u32[]{:S(2)}) collective-permute-start(bf16[512,512]{1,0:T(8,128)(2,1)} %dynamic-slice_bitcast_fusion.4), channel_id=1, source_target_pairs={{0,1},{1,0},{2,3},{3,2},{4,5},{5,4},{6,7},{7,6},{8,9},{9,8},{10,11... | collective-permute-start | bytes 1572872 | tf_op jit(solution)/shard_map/ppermute | solution.py:1316
  9.0 102.1 %collective-permute-start.2 = (bf16[512,512]{1,0:T(8,128)(2,1)}, bf16[512,512]{1,0:T(8,128)(2,1)}, u32[]{:S(2)}, u32[]{:S(2)}) collective-permute-start(bf16[512,512]{1,0:T(8,128)(2,1)} %dynamic-slice_bitcast_fusion.3), channel_id=1, source_target_pairs={{0,1},{1,0},{2,3},{3,2},{4,5},{5,4},{6,7},{7,6},{8,9},{9,8},{10,11... | collective-permute-start | bytes 1572872 | tf_op jit(solution)/shard_map/ppermute | solution.py:1316
  20.9 89.6 %copy-start.27 = (s32[2]{0:T(128)S(1)}, s32[2]{0:T(128)}, u32[]{:S(2)}) copy-start(s32[2]{0:T(128)} %param.29) | copy-start | bytes 28
  20.9 90.2 %copy-start.2 = (bf16[2,512,512]{2,1,0:T(8,128)(2,1)S(1)}, bf16[2,512,512]{2,1,0:T(8,128)(2,1)}, u32[]{:S(2)}) copy-start(bf16[2,512,512]{2,1,0:T(8,128)(2,1)} %param.26) | copy-start | bytes 3145732
  300.8 52.5 %collective-permute-start.5 = (bf16[512,512]{1,0:T(8,128)(2,1)}, bf16[512,512]{1,0:T(8,128)(2,1)}, u32[]{:S(2)}, u32[]{:S(2)}) collective-permute-start(bf16[512,512]{1,0:T(8,128)(2,1)} %dynamic-slice_bitcast_fusion), channel_id=1, source_target_pairs={{0,1},{1,0},{2,3},{3,2},{4,5},{5,4},{6,7},{7,6},{8,9},{9,8},{10,11... | collective-permute-start | bytes 1572872 | tf_op jit(solution)/shard_map/ppermute | solution.py:1329
  301.8 50.6 %copy-start.3 = (bf16[1024,512]{1,0:T(8,128)(2,1)S(1)}, bf16[1024,512]{1,0:T(8,128)(2,1)}, u32[]{:S(2)}) copy-start(bf16[1024,512]{1,0:T(8,128)(2,1)} %get-tuple-element.47) | copy-start | bytes 3145732
  349.1 4.1 copy-start.11
  349.2 4.1 copy-start.12
  349.2 4.1 copy-start.5
  351.1 101.6 %collective-permute-start.4 = (bf16[512,512]{1,0:T(8,128)(2,1)}, bf16[512,512]{1,0:T(8,128)(2,1)}, u32[]{:S(2)}, u32[]{:S(2)}) collective-permute-start(bf16[512,512]{1,0:T(8,128)(2,1)} %dynamic-slice_bitcast_fusion.1), channel_id=1, source_target_pairs={{0,1},{1,0},{2,3},{3,2},{4,5},{5,4},{6,7},{7,6},{8,9},{9,8},{10,11... | collective-permute-start | bytes 1572872 | tf_op jit(solution)/shard_map/ppermute | solution.py:1329
  352.4 106.2 %collective-permute-start.3 = (bf16[512,512]{1,0:T(8,128)(2,1)S(1)}, bf16[512,512]{1,0:T(8,128)(2,1)}, u32[]{:S(2)}, u32[]{:S(2)}) collective-permute-start(bf16[512,512]{1,0:T(8,128)(2,1)S(1)} %dynamic-slice_bitcast_fusion.2), channel_id=1, source_target_pairs={{0,1},{1,0},{2,3},{3,2},{4,5},{5,4},{6,7},{7,6},{8,9},{9,8},{10,11... | collective-permute-start | bytes 1572872 | tf_op jit(solution)/shard_map/ppermute | solution.py:1329
  (2 other events, 7.2 us)
